TPU v7x, 32 devices: a whole 2x2x4 slice. The times are simulated.
32 devices in a mesh: aux: 4 (over z), occ: 8 (over y, x, core).
Axes of the slice: x: 2, y: 2, z: 4, core: 2. Of those that a mesh axis runs over, the one named last changes fastest.
Arguments:
- half_ints: bfloat16 [1024, 128, 1024], P('aux', 'occ'), may hold values from -1 to 1
- block_mask: int32 [16, 128], P('aux', 'occ'), may hold values 0 or 1
- vir_coef: bfloat16 [1024, 2048], replicated, may hold values from -0.1875 to 0.1875
- domains: int32 [128, 512], replicated, may hold values from 0 to 2047, as said below
- vir_energy: float32 [2048], replicated, may hold values from 0.5 to 3
- occ_energy: float32 [128], replicated, may hold values from -3 to -0.5
- pair_count: int32 [8, 4], P('occ', 'aux'), may hold values from 2 to 16, as said below
- pair_code: int32 [8, 4, 16], P('occ', 'aux'), may hold values from 0 to 63, as said below
Outputs:
- density: bfloat16 [1024, 128, 512], P('aux', 'occ')
Inputs may be any that keep to these rules, and one draw needn't show every extreme that they name: `domains`: each row names 512 distinct virtual orbitals. `pair_count`: some block holds exactly 16 live pairs. `pair_code`: the entries of one block's list are distinct.
All inputs are finite; a program needn't handle non-finite values. No bound on the sum of `block_mask` on one device may be relied on, other than what follows from the above.
Results may differ from a plain program's by a relative error of at most 0.0075.
Values may be sent and summed in bfloat16 or wider, within the bound.
No kernel may reach another device: no remote copies, remote signals or barrier semaphores. Data moves between devices by JAX's collectives and lax.ppermute only.
A program may use at most 128 MiB of HBM per device.

v0:
```python
import jax
import jax.numpy as jnp
from jax import lax
from jax.sharding import PartitionSpec as P

BLK = 64
OCC_DEV = 4
PARTNERS = 4


def passed_along(value, axis, steps):
    count = lax.axis_size(axis)
    pairs = [(source, (source + steps) % count) for source in range(count)]
    return lax.ppermute(value, axis, pairs)


def body(half_ints, block_mask, vir_coef, domains, vir_energy, occ_energy, pair_count, pair_code):
    aux_count = lax.axis_size("aux")
    occ_count = lax.axis_size("occ")
    aux_pos = lax.axis_index("aux")
    occ_pos = lax.axis_index("occ")
    local_orbitals = half_ints.shape[1]
    row_mask = jnp.repeat(block_mask, BLK, axis=0).astype(jnp.bfloat16)
    masked = half_ints * row_mask[:, :, None]
    first_orbital = occ_pos * local_orbitals
    own_domains = lax.dynamic_slice_in_dim(domains, first_orbital, local_orbitals, 0)
    gathered_coef = jnp.take(vir_coef, own_domains, axis=1)
    transformed = jnp.einsum(
        "pim,mia->pia", masked, gathered_coef, preferred_element_type=jnp.float32
    ).astype(jnp.bfloat16)
    orbital_ints = lax.all_to_all(transformed, "aux", split_axis=1, concat_axis=0, tiled=True)
    blocks = [orbital_ints]
    current = orbital_ints
    for offset in range(1, PARTNERS):
        current = passed_along(current, "occ", -1)
        blocks.append(current)
    partners = jnp.concatenate(blocks, axis=1)
    dom_rows = []
    occ_rows = []
    for offset in range(PARTNERS):
        start = ((occ_pos + offset) % occ_count * aux_count + aux_pos) * OCC_DEV
        dom_rows.append(lax.dynamic_slice_in_dim(domains, start, OCC_DEV, 0))
        occ_rows.append(lax.dynamic_slice_in_dim(occ_energy, start, OCC_DEV, 0))
    partner_vir = jnp.take(vir_energy, jnp.concatenate(dom_rows, axis=0))
    partner_occ = jnp.concatenate(occ_rows, axis=0)
    live_pairs = pair_count[0, 0]
    codes = pair_code[0, 0]
    span = PARTNERS * OCC_DEV
    gamma = jnp.zeros(orbital_ints.shape, jnp.float32)
    group = min(4, codes.shape[0])
    code_groups = codes.reshape(codes.shape[0] // group, group)
    orbital_iota = jnp.arange(OCC_DEV, dtype=jnp.int32)

    def group_step(index, total):
        group_codes = code_groups[index]
        own_slots = group_codes // span
        partner_slots = group_codes % span
        slot_ids = index * group + jnp.arange(group, dtype=jnp.int32)
        live = (slot_ids < live_pairs).astype(jnp.float32)
        own_rows = jnp.take(partners, own_slots, axis=1)
        partner_rows = jnp.take(partners, partner_slots, axis=1)
        exchange = jnp.einsum(
            "psa,psb->sab", own_rows, partner_rows, preferred_element_type=jnp.float32
        )
        own_vir = jnp.take(partner_vir, own_slots, axis=0)
        other_vir = jnp.take(partner_vir, partner_slots, axis=0)
        occ_sum = jnp.take(partner_occ, own_slots) + jnp.take(partner_occ, partner_slots)
        denom = own_vir[:, :, None] + other_vir[:, None, :] - occ_sum[:, None, None]
        amplitude = (exchange / denom).astype(jnp.bfloat16)
        contrib = jnp.einsum(
            "psb,sab->psa", partner_rows, amplitude, preferred_element_type=jnp.float32
        )
        selector = (orbital_iota[:, None] == own_slots[None, :]).astype(jnp.float32) * live[None, :]
        return total + jnp.einsum(
            "ts,psa->pta", selector, contrib, preferred_element_type=jnp.float32
        )

    gamma = lax.fori_loop(0, code_groups.shape[0], group_step, gamma)
    density = gamma.astype(jnp.bfloat16)
    return lax.all_to_all(density, "aux", split_axis=0, concat_axis=1, tiled=True)


def solution(mesh):
    placed = (
        P("aux", "occ", None),
        P("aux", "occ"),
        P(),
        P(),
        P(),
        P(),
        P("occ", "aux"),
        P("occ", "aux", None),
    )
    return jax.shard_map(
        body, mesh=mesh, in_specs=placed, out_specs=P("aux", "occ", None), check_vma=False
    )
```

profile of v0, /device:TPU:0, one launch (start us, length us, event | category | flops | bytes accessed | tf_op | source)
XLA Modules:
  0.0 646.5 jit_solution(16308331353770401777)
XLA Ops:
  1.6 6.4 copy.13
  8.0 43.5 %gather_fusion.6 = bf16[8192,1024]{1,0:T(8,128)(2,1)} fusion(bf16[1024,2048]{0,1:T(8,128)(2,1)} %copy.13, s32[8192]{0:T(1024)S(1)} %broadcast_clamp_fusion.1), kind=kCustom, calls=%fused_computation.6 | custom fusion | bytes 33587200 | tf_op jit(solution)/shard_map/jit(_take)/gather | solution.py:27
  51.5 7.2 %broadcast_multiply_fusion = bf16[256,16,1024]{2,1,0:T(8,128)(2,1)} fusion(bf16[256,16,1024]{2,1,0:T(8,128)(2,1)} %param.16, bf16[256,16]{1,0:T(8,128)(2,1)S(1)} %bitcast.93), kind=kLoop, calls=%fused_computation.64 | loop fusion | flops 4194304 | bytes 16785408 | tf_op jit(solution)/shard_map/mul | solution.py:24
  58.7 14.3 %convert_bitcast_fusion = bf16[256,16,512]{0,2,1:T(8,128)(2,1)} fusion(bf16[256,16,1024]{2,1,0:T(8,128)(2,1)} %broadcast_multiply_fusion, bf16[16,512,1024]{2,1,0:T(8,128)(2,1)} %bitcast.87, pred[16,512]{1,0:T(8,128)(4,1)S(1)} %compare_and_fusion.2), kind=kOutput, calls=%fused_computation.63 | convolution fusion | flops 4305453056 | bytes 29368320 | tf_op jit(solution)/shard_map/pim,mia->pia/dot_general | solution.py:28
  73.0 99.5 %all_to_all.36 = bf16[256,16,512]{0,2,1:T(8,128)(2,1)S(1)} all-to-all(bf16[256,16,512]{0,2,1:T(8,128)(2,1)} %convert_bitcast_fusion), channel_id=1, replica_groups=mesh['aux'=4,'occ'=8] {'aux'}, dimensions={1} | all-to-all | bytes 8388608 | tf_op jit(solution)/shard_map/all_to_all | solution.py:31
  175.9 46.0 %collective-permute-done = bf16[1024,4,512]{0,2,1:T(8,128)(2,1)S(1)} collective-permute-done((bf16[1024,4,512]{0,2,1:T(8,128)(2,1)S(1)}, bf16[1024,4,512]{0,2,1:T(8,128)(2,1)S(1)}, u32[]{:S(2)}, u32[]{:S(2)}) %collective-permute-start) | collective-permute-done | bytes 4194336 | tf_op jit(solution)/shard_map/ppermute | solution.py:14
  226.7 46.0 %collective-permute-done.1 = bf16[1024,4,512]{0,2,1:T(8,128)(2,1)} collective-permute-done((bf16[1024,4,512]{0,2,1:T(8,128)(2,1)S(1)}, bf16[1024,4,512]{0,2,1:T(8,128)(2,1)}, u32[]{:S(2)}, u32[]{:S(2)}) %collective-permute-start.1) | collective-permute-done | bytes 4194336 | tf_op jit(solution)/shard_map/ppermute | solution.py:14
  276.5 45.5 %gather_fusion.7 = f32[8192]{0:T(1024)S(1)} fusion(f32[2048]{0:T(1024)S(1)} %copy-done, s32[8192]{0:T(1024)S(1)} %broadcast_clamp_fusion), kind=kCustom, calls=%fused_computation.7 | custom fusion | bytes 98304 | tf_op jit(solution)/shard_map/jit(_take)/gather | solution.py:44
  323.6 13.9 %pad_maximum_fusion = bf16[1024,16,512]{0,2,1:T(8,128)(2,1)} fusion(bf16[1024,4,512]{0,2,1:T(8,128)(2,1)} %collective-permute-done.2, bf16[1024,4,512]{0,2,1:T(8,128)(2,1)} %collective-permute-done.1, bf16[1024,4,512]{0,2,1:T(8,128)(2,1)} %copy-done.3, bf16[1024,4,512]{0,2,1:T(8,128)(2,1)} %bitcast.92), kind=kLoop, calls=%fused_computation.55 | loop fusion | flops 25165824 | bytes 33554432 | tf_op jit(solution)/shard_map/concatenate | solution.py:37
  337.5 198.6 %while.16 = (s32[]{:T(128)}, f32[1024,4,512]{2,1,0:T(4,128)}, s32[4,4]{1,0:T(4,128)S(1)}, bf16[1024,16,512]{0,2,1:T(8,128)(2,1)}, f32[16,512]{1,0:T(8,128)S(1)},...) while((s32[]{:T(128)}, f32[1024,4,512]{2,1,0:T(4,128)}, ...), condition=%wide.region_1.5_spmd.clone, body=%wide.region_0.4_spmd.clone.sunk | while | flops 4326430720 | bytes 58810960 | solution.py:78
  340.7 8.5 %gather_fusion.5 = bf16[4,1024,512]{1,2,0:T(8,128)(2,1)} fusion(bf16[1024,16,512]{0,2,1:T(8,128)(2,1)} %get-tuple-element.342, s32[1024]{0:T(1024)S(1)} %pad_clamp_fusion.4), kind=kCustom, calls=%fused_computation.3.clone.clone.1 | custom fusion | bytes 8388624 | tf_op jit(solution)/shard_map/while/body/eval_jaxpr/jit(_take)/gather | solution.py:61
  349.3 8.6 %gather_fusion.4 = bf16[4,1024,512]{1,2,0:T(8,128)(2,1)} fusion(bf16[1024,16,512]{0,2,1:T(8,128)(2,1)} %get-tuple-element.342, s32[1024]{0:T(1024)S(1)} %pad_clamp_fusion.5), kind=kCustom, calls=%fused_computation.clone.clone.1 | custom fusion | bytes 8388624 | tf_op jit(solution)/shard_map/while/body/eval_jaxpr/jit(_take)/gather | solution.py:60
  357.9 11.3 %fusion.60 = bf16[4,512,1024]{2,1,0:T(8,128)(2,1)} fusion(f32[4]{0:T(128)S(1)} %select_add_fusion.2, f32[4,512]{1,0:T(4,128)S(1)} %broadcast_select_fusion.7, f32[4,512]{1,0:T(4,128)S(1)} %broadcast_select_fusion.8, bf16[4,1024,512]{1,2,0:T(8,128)(2,1)} %gather_fusion.4, pred[4]{0:T(512)(128)(4,1)S(1)} %get-tuple-element.317, ...), kind=kOutput, calls=%fused_computation.12.clone.1 | convolution fusion | flops 4305453056 | bytes 12599320 | tf_op jit(solution)/shard_map/while/body/eval_jaxpr/psb,sab->psa/dot_general | solution.py:70
  369.2 7.8 %copy.28 = bf16[4,512,1024]{1,0,2:T(4,128)(2,1)} copy(bf16[4,512,1024]{2,1,0:T(8,128)(2,1)} %fusion.60) | data formatting | bytes 8388608 | tf_op jit(solution)/shard_map/while/body/eval_jaxpr/psb,sab->psa/dot_general | solution.py:70
  377.0 8.2 %bitcast_add_fusion.2 = f32[1024,4,512]{2,1,0:T(4,128)} fusion(f32[1024,4,512]{2,1,0:T(4,128)} %get-tuple-element.330, bf16[4,512,1024]{1,0,2:T(4,128)(2,1)} %copy.28, pred[]{:T(512)S(6)} %compare.28, bf16[4]{0:T(256)(128)(2,1)S(1)} %get-tuple-element.318, s32[4]{0:T(128)S(1)} %fusion.61), kind=kOutput, calls=%fused_computation.9.clone.1 | convolution fusion | flops 20971552 | bytes 20971544 | tf_op jit(solution)/shard_map/while/body/eval_jaxpr/ts,psa->pta/dot_general | solution.py:74
  388.5 8.5 %gather_fusion.5 = bf16[4,1024,512]{1,2,0:T(8,128)(2,1)} fusion(bf16[1024,16,512]{0,2,1:T(8,128)(2,1)} %get-tuple-element.342, s32[1024]{0:T(1024)S(1)} %pad_clamp_fusion.4), kind=kCustom, calls=%fused_computation.3.clone.clone.1 | custom fusion | bytes 8388624 | tf_op jit(solution)/shard_map/while/body/eval_jaxpr/jit(_take)/gather | solution.py:61
  397.1 8.6 %gather_fusion.4 = bf16[4,1024,512]{1,2,0:T(8,128)(2,1)} fusion(bf16[1024,16,512]{0,2,1:T(8,128)(2,1)} %get-tuple-element.342, s32[1024]{0:T(1024)S(1)} %pad_clamp_fusion.5), kind=kCustom, calls=%fused_computation.clone.clone.1 | custom fusion | bytes 8388624 | tf_op jit(solution)/shard_map/while/body/eval_jaxpr/jit(_take)/gather | solution.py:60
  405.7 11.3 %fusion.60 = bf16[4,512,1024]{2,1,0:T(8,128)(2,1)} fusion(f32[4]{0:T(128)S(1)} %select_add_fusion.2, f32[4,512]{1,0:T(4,128)S(1)} %broadcast_select_fusion.7, f32[4,512]{1,0:T(4,128)S(1)} %broadcast_select_fusion.8, bf16[4,1024,512]{1,2,0:T(8,128)(2,1)} %gather_fusion.4, pred[4]{0:T(512)(128)(4,1)S(1)} %get-tuple-element.317, ...), kind=kOutput, calls=%fused_computation.12.clone.1 | convolution fusion | flops 4305453056 | bytes 12599320 | tf_op jit(solution)/shard_map/while/body/eval_jaxpr/psb,sab->psa/dot_general | solution.py:70
  417.0 7.8 %copy.28 = bf16[4,512,1024]{1,0,2:T(4,128)(2,1)} copy(bf16[4,512,1024]{2,1,0:T(8,128)(2,1)} %fusion.60) | data formatting | bytes 8388608 | tf_op jit(solution)/shard_map/while/body/eval_jaxpr/psb,sab->psa/dot_general | solution.py:70
  424.8 10.7 %bitcast_add_fusion.2 = f32[1024,4,512]{2,1,0:T(4,128)} fusion(f32[1024,4,512]{2,1,0:T(4,128)} %get-tuple-element.330, bf16[4,512,1024]{1,0,2:T(4,128)(2,1)} %copy.28, pred[]{:T(512)S(6)} %compare.28, bf16[4]{0:T(256)(128)(2,1)S(1)} %get-tuple-element.318, s32[4]{0:T(128)S(1)} %fusion.61), kind=kOutput, calls=%fused_computation.9.clone.1 | convolution fusion | flops 20971552 | bytes 20971544 | tf_op jit(solution)/shard_map/while/body/eval_jaxpr/ts,psa->pta/dot_general | solution.py:74
  438.8 8.5 %gather_fusion.5 = bf16[4,1024,512]{1,2,0:T(8,128)(2,1)} fusion(bf16[1024,16,512]{0,2,1:T(8,128)(2,1)} %get-tuple-element.342, s32[1024]{0:T(1024)S(1)} %pad_clamp_fusion.4), kind=kCustom, calls=%fused_computation.3.clone.clone.1 | custom fusion | bytes 8388624 | tf_op jit(solution)/shard_map/while/body/eval_jaxpr/jit(_take)/gather | solution.py:61
  447.3 8.6 %gather_fusion.4 = bf16[4,1024,512]{1,2,0:T(8,128)(2,1)} fusion(bf16[1024,16,512]{0,2,1:T(8,128)(2,1)} %get-tuple-element.342, s32[1024]{0:T(1024)S(1)} %pad_clamp_fusion.5), kind=kCustom, calls=%fused_computation.clone.clone.1 | custom fusion | bytes 8388624 | tf_op jit(solution)/shard_map/while/body/eval_jaxpr/jit(_take)/gather | solution.py:60
  455.9 11.3 %fusion.60 = bf16[4,512,1024]{2,1,0:T(8,128)(2,1)} fusion(f32[4]{0:T(128)S(1)} %select_add_fusion.2, f32[4,512]{1,0:T(4,128)S(1)} %broadcast_select_fusion.7, f32[4,512]{1,0:T(4,128)S(1)} %broadcast_select_fusion.8, bf16[4,1024,512]{1,2,0:T(8,128)(2,1)} %gather_fusion.4, pred[4]{0:T(512)(128)(4,1)S(1)} %get-tuple-element.317, ...), kind=kOutput, calls=%fused_computation.12.clone.1 | convolution fusion | flops 4305453056 | bytes 12599320 | tf_op jit(solution)/shard_map/while/body/eval_jaxpr/psb,sab->psa/dot_general | solution.py:70
  467.3 7.8 %copy.28 = bf16[4,512,1024]{1,0,2:T(4,128)(2,1)} copy(bf16[4,512,1024]{2,1,0:T(8,128)(2,1)} %fusion.60) | data formatting | bytes 8388608 | tf_op jit(solution)/shard_map/while/body/eval_jaxpr/psb,sab->psa/dot_general | solution.py:70
  475.1 10.7 %bitcast_add_fusion.2 = f32[1024,4,512]{2,1,0:T(4,128)} fusion(f32[1024,4,512]{2,1,0:T(4,128)} %get-tuple-element.330, bf16[4,512,1024]{1,0,2:T(4,128)(2,1)} %copy.28, pred[]{:T(512)S(6)} %compare.28, bf16[4]{0:T(256)(128)(2,1)S(1)} %get-tuple-element.318, s32[4]{0:T(128)S(1)} %fusion.61), kind=kOutput, calls=%fused_computation.9.clone.1 | convolution fusion | flops 20971552 | bytes 20971544 | tf_op jit(solution)/shard_map/while/body/eval_jaxpr/ts,psa->pta/dot_general | solution.py:74
  489.1 8.5 %gather_fusion.5 = bf16[4,1024,512]{1,2,0:T(8,128)(2,1)} fusion(bf16[1024,16,512]{0,2,1:T(8,128)(2,1)} %get-tuple-element.342, s32[1024]{0:T(1024)S(1)} %pad_clamp_fusion.4), kind=kCustom, calls=%fused_computation.3.clone.clone.1 | custom fusion | bytes 8388624 | tf_op jit(solution)/shard_map/while/body/eval_jaxpr/jit(_take)/gather | solution.py:61
  497.6 8.6 %gather_fusion.4 = bf16[4,1024,512]{1,2,0:T(8,128)(2,1)} fusion(bf16[1024,16,512]{0,2,1:T(8,128)(2,1)} %get-tuple-element.342, s32[1024]{0:T(1024)S(1)} %pad_clamp_fusion.5), kind=kCustom, calls=%fused_computation.clone.clone.1 | custom fusion | bytes 8388624 | tf_op jit(solution)/shard_map/while/body/eval_jaxpr/jit(_take)/gather | solution.py:60
  506.2 11.3 %fusion.60 = bf16[4,512,1024]{2,1,0:T(8,128)(2,1)} fusion(f32[4]{0:T(128)S(1)} %select_add_fusion.2, f32[4,512]{1,0:T(4,128)S(1)} %broadcast_select_fusion.7, f32[4,512]{1,0:T(4,128)S(1)} %broadcast_select_fusion.8, bf16[4,1024,512]{1,2,0:T(8,128)(2,1)} %gather_fusion.4, pred[4]{0:T(512)(128)(4,1)S(1)} %get-tuple-element.317, ...), kind=kOutput, calls=%fused_computation.12.clone.1 | convolution fusion | flops 4305453056 | bytes 12599320 | tf_op jit(solution)/shard_map/while/body/eval_jaxpr/psb,sab->psa/dot_general | solution.py:70
  517.5 7.8 %copy.28 = bf16[4,512,1024]{1,0,2:T(4,128)(2,1)} copy(bf16[4,512,1024]{2,1,0:T(8,128)(2,1)} %fusion.60) | data formatting | bytes 8388608 | tf_op jit(solution)/shard_map/while/body/eval_jaxpr/psb,sab->psa/dot_general | solution.py:70
  525.4 10.7 %bitcast_add_fusion.2 = f32[1024,4,512]{2,1,0:T(4,128)} fusion(f32[1024,4,512]{2,1,0:T(4,128)} %get-tuple-element.330, bf16[4,512,1024]{1,0,2:T(4,128)(2,1)} %copy.28, pred[]{:T(512)S(6)} %compare.28, bf16[4]{0:T(256)(128)(2,1)S(1)} %get-tuple-element.318, s32[4]{0:T(128)S(1)} %fusion.61), kind=kOutput, calls=%fused_computation.9.clone.1 | convolution fusion | flops 20971552 | bytes 20971544 | tf_op jit(solution)/shard_map/while/body/eval_jaxpr/ts,psa->pta/dot_general | solution.py:74
  540.9 94.4 %all_to_all.37 = bf16[1024,4,512]{2,1,0:T(4,128)(2,1)S(1)} all-to-all(bf16[1024,4,512]{2,1,0:T(4,128)(2,1)S(1)} %convert_element_type.51), channel_id=1, replica_groups=mesh['aux'=4,'occ'=8] {'aux'}, dimensions={0} | all-to-all | bytes 8388608 | tf_op jit(solution)/shard_map/all_to_all | solution.py:80
  639.6 6.9 %all_to_all.33 = bf16[256,16,512]{2,1,0:T(8,128)(2,1)} reshape(bf16[256,4,4,512]{3,2,1,0:T(4,128)(2,1)} %bitcast.90) | data formatting | bytes 8388608 | tf_op jit(solution)/shard_map/all_to_all | solution.py:80
  (87 shorter events, 37.2 us)
Async XLA Ops:
  0.0 276.5 %copy-start = (f32[2048]{0:T(1024)S(1)}, f32[2048]{0:T(1024)}, u32[]{:S(2)}) copy-start(f32[2048]{0:T(1024)} %param.20) | copy-start | bytes 24580
  1.6 6.4 copy-start.5
  173.1 2.1 copy-start.2
  175.1 46.8 %collective-permute-start = (bf16[1024,4,512]{0,2,1:T(8,128)(2,1)S(1)}, bf16[1024,4,512]{0,2,1:T(8,128)(2,1)S(1)}, u32[]{:S(2)}, u32[]{:S(2)}) collective-permute-start(bf16[1024,4,512]{0,2,1:T(8,128)(2,1)S(1)} %bitcast.91), channel_id=1, source_target_pairs={{0,7},{1,0},{2,1},{3,2},{4,3},{5,4},{6,5},{7,6},{8,15},{9,8},{10,9... | collective-permute-start | bytes 12582920 | tf_op jit(solution)/shard_map/ppermute | solution.py:14
  221.9 2.0 copy-start.3
  223.9 48.8 %collective-permute-start.1 = (bf16[1024,4,512]{0,2,1:T(8,128)(2,1)S(1)}, bf16[1024,4,512]{0,2,1:T(8,128)(2,1)}, u32[]{:S(2)}, u32[]{:S(2)}) collective-permute-start(bf16[1024,4,512]{0,2,1:T(8,128)(2,1)S(1)} %collective-permute-done), channel_id=1, source_target_pairs={{0,7},{1,0},{2,1},{3,2},{4,3},{5,4},{6,5},{7,6},{8,15},{9,8},{10,9... | collective-permute-start | bytes 12582920 | tf_op jit(solution)/shard_map/ppermute | solution.py:14
  272.8 50.8 %collective-permute-start.2 = (bf16[1024,4,512]{0,2,1:T(8,128)(2,1)}, bf16[1024,4,512]{0,2,1:T(8,128)(2,1)}, u32[]{:S(2)}, u32[]{:S(2)}) collective-permute-start(bf16[1024,4,512]{0,2,1:T(8,128)(2,1)} %collective-permute-done.1), channel_id=1, source_target_pairs={{0,7},{1,0},{2,1},{3,2},{4,3},{5,4},{6,5},{7,6},{8,15},{9,8},{10,9... | collective-permute-start | bytes 12582920 | tf_op jit(solution)/shard_map/ppermute | solution.py:14
  276.5 46.1 %copy-start.6 = (s32[1,1,16]{2,1,0:T(1,128)S(1)}, s32[1,1,16]{2,1,0:T(1,128)}, u32[]{:S(2)}) copy-start(s32[1,1,16]{2,1,0:T(1,128)} %param.23) | copy-start | bytes 196
  276.5 46.8 %copy-start.4 = (f32[128]{0:T(128)S(1)}, f32[128]{0:T(128)}, u32[]{:S(2)}) copy-start(f32[128]{0:T(128)} %param.21) | copy-start | bytes 1540
  639.6 6.9 %copy-start.1 = (f32[2048]{0:T(1024)S(1)}, f32[2048]{0:T(1024)}, u32[]{:S(2)}) copy-start(f32[2048]{0:T(1024)} %param.20) | copy-start | bytes 24580
where the time goes:
time: 648 us; the launch traced here: 647 us
  local copies, waits for them, and re-layouts  222 us (34%)
  blocking collectives  194 us (30%)
  matrix products  99.9 us (15%)
  waiting for transfers between devices  92 us (14%)
  other arithmetic  31.7 us (5%)
    all_to_all x1, blocking collectives, body(): lax.all_to_all(transformed, 'aux', split_axis=1, concat_axis=0, tiled=True)  99.5 us
    all_to_all x1, blocking collectives, body(): lax.all_to_all(density, 'aux', split_axis=0, concat_axis=1, tiled=True)  94.4 us
    ppermute x3, waiting for transfers between devices, passed_along(): return lax.ppermute(value, axis, pairs)  92 us
    gather x2, local copies, waits for them, and re-layouts, body(): partner_vir = jnp.take(vir_energy, jnp.concatenate(dom_rows, axis=0))  45.5 us
    dot_general x4, matrix products, group_step(): jnp.einsum('psb,sab->psa', partner_rows, amplitude, preferred_element_typ...  45.3 us
    gather x1, local copies, waits for them, and re-layouts, body(): gathered_coef = jnp.take(vir_coef, own_domains, axis=1)  43.5 us
    dot_general x4, matrix products, group_step(): jnp.einsum('ts,psa->pta', selector, contrib, preferred_element_type=jnp.f...  40.3 us
    gather x4, local copies, waits for them, and re-layouts, group_step(): own_rows = jnp.take(partners, own_slots, axis=1)  34.4 us
  transfers between devices with their start and end apart: 3, of which 2 were waited for; matrix products, arithmetic and copies ran while one was open for 7% of the time, Pallas kernels for 0%

commit v1 on v0

v1 whole, which is shorter than its diff:
```python
import functools

import jax
import jax.numpy as jnp
from jax import lax
from jax.experimental import pallas as pl
from jax.experimental.pallas import tpu as pltpu
from jax.sharding import PartitionSpec as P

BLK = 64
OCC_DEV = 4
PARTNERS = 4
ROWS = 16
MIB = 1024 * 1024


def sort_kernel(orbitals, x_ref, mask_ref, out_ref):
    width = orbitals * ROWS
    block = x_ref.shape[0]
    row = lax.broadcasted_iota(jnp.int32, (width, width), 0)
    col = lax.broadcasted_iota(jnp.int32, (width, width), 1)
    hit = (row // ROWS == col % orbitals) & (row % ROWS == col // orbitals)
    for part in range(block // ROWS):
        spread = jnp.where(hit, mask_ref[part : part + 1, :], 0.0).astype(jnp.bfloat16)
        rows = x_ref[part * ROWS : (part + 1) * ROWS].reshape(width, x_ref.shape[2])
        moved = jnp.dot(spread, rows, preferred_element_type=jnp.float32).astype(jnp.bfloat16)
        out_ref[:, part * ROWS : (part + 1) * ROWS, :] = moved.reshape(orbitals, ROWS, -1)


def sorted_rows(half_ints, block_mask):
    rows, orbitals, basis = half_ints.shape
    block = 4 * ROWS
    width = orbitals * ROWS
    mask = jnp.repeat(block_mask, BLK // ROWS, axis=0).astype(jnp.float32)
    mask = jnp.tile(mask, (1, ROWS))
    steps = rows // block
    mask = mask.reshape(steps, block // ROWS, width)
    return pl.pallas_call(
        functools.partial(sort_kernel, orbitals),
        grid=(steps,),
        in_specs=[
            pl.BlockSpec((block, orbitals, basis), lambda g: (g, 0, 0)),
            pl.BlockSpec((None, block // ROWS, width), lambda g: (g, 0, 0)),
        ],
        out_specs=pl.BlockSpec((orbitals, block, basis), lambda g: (0, g, 0)),
        out_shape=jax.ShapeDtypeStruct((orbitals, rows, basis), jnp.bfloat16),
        compiler_params=pltpu.CompilerParams(vmem_limit_bytes=40 * MIB),
        cost_estimate=pl.CostEstimate(
            flops=2 * rows * orbitals * basis * width,
            bytes_accessed=4 * rows * orbitals * basis,
            transcendentals=0,
        ),
        name="sort_rows",
    )(half_ints, mask)


def transform_kernel(count, pos_ref, x_ref, dom_ref, coef_ref, *out_refs):
    step = pl.program_id(0)
    tile = 512
    whole = coef_ref.shape[1]
    dom = dom_ref[...]
    total = None
    for part in range(whole // tile):
        full = jnp.dot(
            x_ref[...], coef_ref[:, part * tile : (part + 1) * tile], preferred_element_type=jnp.float32
        ).astype(jnp.bfloat16)
        row = lax.broadcasted_iota(jnp.int32, (tile, dom.shape[1]), 0) + part * tile
        pick = jnp.where(row == dom, 1.0, 0.0).astype(jnp.bfloat16)
        term = jnp.dot(full, pick, preferred_element_type=jnp.float32)
        total = term if total is None else total + term
    total = total.astype(jnp.bfloat16)
    for index in range(count):
        @pl.when(step == index)
        def _():
            out_refs[index][...] = total


def transformed(rows_of, own_domains, vir_coef, aux_pos, chunk, count):
    orbitals, rows, basis = rows_of.shape
    virs = own_domains.shape[2]
    whole = vir_coef.shape[1]

    def orbital(step, pos_ref):
        return lax.rem(pos_ref[0] + step, count) * OCC_DEV + chunk

    return pl.pallas_call(
        functools.partial(transform_kernel, count),
        grid_spec=pltpu.PrefetchScalarGridSpec(
            num_scalar_prefetch=1,
            grid=(count,),
            in_specs=[
                pl.BlockSpec((None, rows, basis), lambda g, pos: (orbital(g, pos), 0, 0)),
                pl.BlockSpec((None, 1, virs), lambda g, pos: (orbital(g, pos), 0, 0)),
                pl.BlockSpec((basis, whole), lambda g, pos: (0, 0), pipeline_mode=pl.Buffered(1)),
            ],
            out_specs=[pl.BlockSpec((rows, virs), lambda g, pos: (0, 0)) for _ in range(count)],
        ),
        out_shape=[jax.ShapeDtypeStruct((rows, virs), jnp.bfloat16) for _ in range(count)],
        compiler_params=pltpu.CompilerParams(vmem_limit_bytes=40 * MIB),
        cost_estimate=pl.CostEstimate(
            flops=2 * count * rows * whole * (basis + virs),
            bytes_accessed=2 * (count * rows * (basis + virs) + basis * whole),
            transcendentals=0,
        ),
        name="transform",
    )(aux_pos, rows_of, own_domains, vir_coef)


def pair_kernel(chunk, count, live_ref, code_ref, odd_ref, occ_ref, own_ref, col_ref, row_ref, *refs):
    kinds = 5
    blocks = refs[: kinds * OCC_DEV]
    outs = refs[kinds * OCC_DEV : kinds * OCC_DEV + count]
    turned, total, held, sems, todo = refs[kinds * OCC_DEV + count :]
    span = PARTNERS * OCC_DEV
    slots = code_ref.shape[0]
    odd = odd_ref[0]

    def scan(slot, found):
        code = code_ref[slot]
        mine = (slot < live_ref[0]) & (code // span == chunk)

        @pl.when(mine)
        def _():
            todo[found] = code % span

        return found + mine.astype(jnp.int32)

    pairs = lax.fori_loop(0, slots, scan, jnp.int32(0))

    def source(slot):
        offset = slot // OCC_DEV
        one = jnp.where(odd == 1, 3, 1)
        three = jnp.where(odd == 1, 4, 3)
        kind = jnp.where(offset == 0, 0, jnp.where(offset == 1, one, jnp.where(offset == 2, 2, three)))
        return kind * OCC_DEV + slot % OCC_DEV

    def fetch(index):
        place = source(todo[index])
        buffer = lax.rem(index, 2)
        for number, block in enumerate(blocks):
            @pl.when(place == number)
            def _():
                pltpu.make_async_copy(block, held.at[buffer], sems.at[buffer]).start()

    @pl.when(pairs > 0)
    def _():
        fetch(0)
        turned[...] = own_ref[...].T

    total[...] = jnp.zeros_like(total)

    def step(index, carry):
        @pl.when(index + 1 < pairs)
        def _():
            fetch(index + 1)

        buffer = lax.rem(index, 2)
        pltpu.make_async_copy(blocks[0], held.at[buffer], sems.at[buffer]).wait()
        slot = todo[index]
        shift = occ_ref[chunk] + occ_ref[slot]
        other = held[buffer]
        exchange = jnp.dot(turned[...], other, preferred_element_type=jnp.float32)
        denom = (col_ref[...] + row_ref[slot]) - shift
        amplitude = (exchange / denom).astype(jnp.bfloat16)
        total[...] += lax.dot_general(
            other, amplitude, (((1,), (1,)), ((), ())), preferred_element_type=jnp.float32
        )
        return carry

    lax.fori_loop(0, pairs, step, jnp.int32(0))
    rows = outs[0].shape[0]
    for index, out in enumerate(outs):
        out[...] = total[index * rows : (index + 1) * rows, :].astype(jnp.bfloat16)


def densities(chunk, count, live, codes, odd, partner_occ, own, own_vir, vir_rows, blocks):
    aux, virs = own.shape
    rows = aux // count
    whole = lambda shape: pl.BlockSpec(shape, lambda: (0,) * len(shape))
    smem = pl.BlockSpec(memory_space=pltpu.SMEM)
    return pl.pallas_call(
        functools.partial(pair_kernel, chunk, count),
        in_specs=[smem, smem, smem, smem, whole(own.shape), whole(own_vir.shape), whole(vir_rows.shape)]
        + [pl.BlockSpec(memory_space=pl.ANY)] * len(blocks),
        out_specs=[whole((rows, virs))] * count,
        out_shape=[jax.ShapeDtypeStruct((rows, virs), jnp.bfloat16)] * count,
        scratch_shapes=[
            pltpu.VMEM((virs, aux), jnp.bfloat16),
            pltpu.VMEM((aux, virs), jnp.float32),
            pltpu.VMEM((2, aux, virs), jnp.bfloat16),
            pltpu.SemaphoreType.DMA((2,)),
            pltpu.SMEM((codes.shape[0],), jnp.int32),
        ],
        compiler_params=pltpu.CompilerParams(vmem_limit_bytes=40 * MIB),
        cost_estimate=pl.CostEstimate(
            flops=4 * 4 * aux * virs * virs, bytes_accessed=6 * aux * virs, transcendentals=0
        ),
        name="pairs",
    )(live, codes, odd, partner_occ, own, own_vir, vir_rows, *blocks)


def spread_kernel(count, pos_ref, *refs):
    pieces, out = refs[:-1], refs[-1]
    orbitals = count * OCC_DEV
    width = orbitals * ROWS
    row = lax.broadcasted_iota(jnp.int32, (width, width), 0)
    col = lax.broadcasted_iota(jnp.int32, (width, width), 1)
    group = col // ROWS
    place = lax.rem(pos_ref[0] + group % count, count) * OCC_DEV + group // count
    hit = jnp.where((row % orbitals == place) & (row // orbitals == col % ROWS), 1.0, 0.0).astype(jnp.bfloat16)
    for part in range(out.shape[0] // ROWS):
        span = pl.ds(part * ROWS, ROWS)
        rows = jnp.concatenate([piece[span, :] for piece in pieces], axis=0)
        moved = jnp.dot(hit, rows, preferred_element_type=jnp.float32).astype(jnp.bfloat16)
        out[span] = moved.reshape(ROWS, orbitals, -1)


def assembled(pieces, aux_pos, count):
    rows, virs = pieces[0].shape
    orbitals = count * OCC_DEV
    block = 4 * ROWS
    return pl.pallas_call(
        functools.partial(spread_kernel, count),
        grid_spec=pltpu.PrefetchScalarGridSpec(
            num_scalar_prefetch=1,
            grid=(rows // block,),
            in_specs=[pl.BlockSpec((block, virs), lambda g, pos: (g, 0))] * len(pieces),
            out_specs=pl.BlockSpec((block, orbitals, virs), lambda g, pos: (g, 0, 0)),
        ),
        out_shape=jax.ShapeDtypeStruct((rows, orbitals, virs), jnp.bfloat16),
        compiler_params=pltpu.CompilerParams(vmem_limit_bytes=40 * MIB),
        cost_estimate=pl.CostEstimate(
            flops=2 * rows * orbitals * virs * orbitals * ROWS,
            bytes_accessed=4 * rows * orbitals * virs,
            transcendentals=0,
        ),
        name="assemble",
    )(aux_pos, *pieces)


def body(half_ints, block_mask, vir_coef, domains, vir_energy, occ_energy, pair_count, pair_code):
    aux_count = lax.axis_size("aux")
    occ_count = lax.axis_size("occ")
    aux_pos = lax.axis_index("aux")
    occ_pos = lax.axis_index("occ")
    local_orbitals = half_ints.shape[1]
    pos = aux_pos.astype(jnp.int32).reshape(1)
    odd = (occ_pos % 2).astype(jnp.int32).reshape(1)

    def along_aux(value, steps):
        return lax.ppermute(value, "aux", [(z, (z + steps) % aux_count) for z in range(aux_count)])

    rows_of = sorted_rows(half_ints, block_mask)
    own_domains = lax.dynamic_slice_in_dim(domains, occ_pos * local_orbitals, local_orbitals, 0)
    own_domains = own_domains[:, None, :]

    dom_rows = []
    occ_rows = []
    for offset in range(PARTNERS):
        start = ((occ_pos + offset) % occ_count * aux_count + aux_pos) * OCC_DEV
        dom_rows.append(lax.dynamic_slice_in_dim(domains, start, OCC_DEV, 0))
        occ_rows.append(lax.dynamic_slice_in_dim(occ_energy, start, OCC_DEV, 0))
    partner_vir = jnp.take(vir_energy, jnp.concatenate(dom_rows, axis=0))
    partner_occ = jnp.concatenate(occ_rows, axis=0)

    twin = [(n, n ^ 1) for n in range(occ_count)]
    next_chip = [(n, (n - 2) % occ_count) for n in range(occ_count)]
    third = [((n + 3) % occ_count, n) for n in range(1, occ_count, 2)]
    own, swap, chip, cross, far = [], [], [], [], []
    for chunk in range(OCC_DEV):
        pieces = transformed(rows_of, own_domains, vir_coef, pos, chunk, aux_count)
        pieces = [pieces[0]] + [along_aux(pieces[step], step) for step in range(1, aux_count)]
        orbital = jnp.concatenate(pieces, axis=0)
        own.append(orbital)
        swap.append(lax.ppermute(orbital, "occ", twin))
        chip.append(lax.ppermute(orbital, "occ", next_chip))
        cross.append(lax.ppermute(chip[-1], "occ", twin))
        far.append(lax.ppermute(orbital, "occ", third))
    blocks = own + swap + chip + cross + far
    live = pair_count[0]
    codes = pair_code[0, 0]
    results = []
    for chunk in range(OCC_DEV):
        pieces = densities(
            chunk, aux_count, live, codes, odd, partner_occ, own[chunk],
            partner_vir[chunk][:, None], partner_vir[:, None, :], blocks,
        )
        results += [pieces[0]] + [along_aux(pieces[step], -step) for step in range(1, aux_count)]
    return assembled(results, pos, aux_count)


def solution(mesh):
    placed = (
        P("aux", "occ", None),
        P("aux", "occ"),
        P(),
        P(),
        P(),
        P(),
        P("occ", "aux"),
        P("occ", "aux", None),
    )
    return jax.shard_map(
        body, mesh=mesh, in_specs=placed, out_specs=P("aux", "occ", None), check_vma=False
    )
```

time: 648 us -> 353 us (0.54)
  blocking collectives: 194 us -> 0 us
  local copies, waits for them, and re-layouts: 222 us -> 60.8 us
  matrix products: 99.9 us -> 0 us
  starting transfers between devices: 6.47 us -> 88 us
  Pallas kernels: 0 us -> 65.7 us
  waiting for transfers between devices: 92 us -> 133 us
  other arithmetic: 31.7 us -> 0.89 us
    all_to_all x2 -> x0, blocking collectives: 194 us -> none  [the longest x1 99.5 us: body(): lax.all_to_all(transformed, 'aux', split_axis=1, concat_axis=0, tiled=True)]
    gather x25 -> x0, local copies, waits for them, and re-layouts: 122 us -> none  [the longest x1 43.5 us: body(): gathered_coef = jnp.take(vir_coef, own_domains, axis=1)]
    dot_general x9 -> x0, matrix products: 99.9 us -> none  [the longest x4 45.3 us: group_step(): jnp.einsum('psb,sab->psa', partner_rows, amplitude, preferred_element_typ...]
    ppermute x3 -> x40, starting transfers between devices: 6.47 us -> 88 us  [the longest x24 66.1 us: along_aux(): lax.ppermute(value, 'aux', [(z, (z + steps) % aux_count) for z in range(a...]
    pallas_call x0 -> x10, Pallas kernels: none -> 65.7 us  [the longest x4 33.4 us: transformed(): pl.pallas_call(functools.partial(transform_kernel, count), grid_spec=pltp...]
    ppermute x3 -> x40, waiting for transfers between devices: 92 us -> 133 us  [the longest x24 77 us: along_aux(): lax.ppermute(value, 'aux', [(z, (z + steps) % aux_count) for z in range(a...]
    dot_general x4 -> x0, local copies, waits for them, and re-layouts: 31.3 us -> none  [group_step(): jnp.einsum('psb,sab->psa', partner_rows, amplitude, preferred_element_typ...]
    concatenate x1 -> x0, other arithmetic: 13.9 us -> none  [body(): partners = jnp.concatenate(blocks, axis=1)]
  transfers between devices with their start and end apart: 3 -> 40, of which waited for: 2 -> 12; matrix products, arithmetic and copies ran while one was open for 7% -> 14% of each run, Pallas kernels for 0% -> 12%
where the time goes in v1:
time: 353 us; the launch traced here: 349 us
  waiting for transfers between devices  133 us (38%)
  starting transfers between devices  88 us (25%)
  Pallas kernels  65.7 us (19%)
  local copies, waits for them, and re-layouts  60.8 us (17%)
    ppermute x24, waiting for transfers between devices, along_aux(): lax.ppermute(value, 'aux', [(z, (z + steps) % aux_count) for z in range(a...  77 us
    ppermute x24, starting transfers between devices, along_aux(): lax.ppermute(value, 'aux', [(z, (z + steps) % aux_count) for z in range(a...  66.1 us
    ppermute x4, waiting for transfers between devices, body(): chip.append(lax.ppermute(orbital, 'occ', next_chip))  49.2 us
    gather x2, local copies, waits for them, and re-layouts, body(): partner_vir = jnp.take(vir_energy, jnp.concatenate(dom_rows, axis=0))  45.5 us
    pallas_call x4, Pallas kernels, transformed(): pl.pallas_call(functools.partial(transform_kernel, count), grid_spec=pltp...  33.4 us
    pallas_call x4, Pallas kernels, densities(): pl.pallas_call(functools.partial(pair_kernel, chunk, count), in_specs=[sm...  22.9 us
    ppermute x4, starting transfers between devices, body(): far.append(lax.ppermute(orbital, 'occ', third))  12.8 us
    unnamed x56, local copies, waits for them, and re-layouts  10.6 us
  transfers between devices with their start and end apart: 40, of which 12 were waited for; matrix products, arithmetic and copies ran while one was open for 14% of the time, Pallas kernels for 12%

profile of v1, /device:TPU:0, one launch (start us, length us, event | category | flops | bytes accessed | tf_op | source)
XLA Modules:
  0.0 349.3 jit_solution(2411624445876265461)
XLA Ops:
  1.6 6.1 %sort_rows.1.x_ref = bf16[16,256,1024]{2,1,0:T(8,128)(2,1)S(1)} custom-call(bf16[256,16,1024]{2,1,0:T(8,128)(2,1)} %x_ref.1, f32[4,4,256]{2,1,0:T(4,128)S(1)} %tile.9.mask_ref), custom_call_target="tpu_custom_call" | custom-call | flops 2147483648 | bytes 16777216 | tf_op jit(solution)/shard_map/sort_rows/pallas_call | solution.py:38
  7.7 8.4 %transform.7 = (bf16[256,512]{1,0:T(8,128)(2,1)S(1)}, bf16[256,512]{1,0:T(8,128)(2,1)S(1)}, bf16[256,512]{1,0:T(8,128)(2,1)S(1)}, bf16[256,512]{1,0:T(8,128)(2,1)S(1)}) custom-call(s32[1]{0:T(128)} %bitcast.pos_ref, bf16[16,256,1024]{2,1,0:T(8,128)(2,1)S(1)} %sort_rows.1.x_ref, s32[16,1,512]{2,1,0:T(1,128)S(1)} %broadcast_in_dim.19.dom_ref, ...), custom_call_target="tpu_custom_call" | custom-call | flops 6442450944 | bytes 7340032 | tf_op jit(solution)/shard_map/transform/pallas_call | solution.py:86
  16.1 3.1 collective-permute-start.9
  23.1 8.4 %transform.6 = (bf16[256,512]{1,0:T(8,128)(2,1)S(1)}, bf16[256,512]{1,0:T(8,128)(2,1)S(1)}, bf16[256,512]{1,0:T(8,128)(2,1)S(1)}, bf16[256,512]{1,0:T(8,128)(2,1)S(1)}) custom-call(s32[1]{0:T(128)} %bitcast.pos_ref, bf16[16,256,1024]{2,1,0:T(8,128)(2,1)S(1)} %sort_rows.1.x_ref, s32[16,1,512]{2,1,0:T(1,128)S(1)} %broadcast_in_dim.19.dom_ref, ...), custom_call_target="tpu_custom_call" | custom-call | flops 6442450944 | bytes 7340032 | tf_op jit(solution)/shard_map/transform/pallas_call | solution.py:86
  32.5 8.3 %transform.5 = (bf16[256,512]{1,0:T(8,128)(2,1)S(1)}, bf16[256,512]{1,0:T(8,128)(2,1)S(1)}, bf16[256,512]{1,0:T(8,128)(2,1)S(1)}, bf16[256,512]{1,0:T(8,128)(2,1)S(1)}) custom-call(s32[1]{0:T(128)} %bitcast.pos_ref, bf16[16,256,1024]{2,1,0:T(8,128)(2,1)S(1)} %sort_rows.1.x_ref, s32[16,1,512]{2,1,0:T(1,128)S(1)} %broadcast_in_dim.19.dom_ref, ...), custom_call_target="tpu_custom_call" | custom-call | flops 6442450944 | bytes 7340032 | tf_op jit(solution)/shard_map/transform/pallas_call | solution.py:86
  40.9 8.4 %transform.4 = (bf16[256,512]{1,0:T(8,128)(2,1)S(1)}, bf16[256,512]{1,0:T(8,128)(2,1)S(1)}, bf16[256,512]{1,0:T(8,128)(2,1)S(1)}, bf16[256,512]{1,0:T(8,128)(2,1)S(1)}) custom-call(s32[1]{0:T(128)} %bitcast.pos_ref, bf16[16,256,1024]{2,1,0:T(8,128)(2,1)S(1)} %sort_rows.1.x_ref, s32[16,1,512]{2,1,0:T(1,128)S(1)} %broadcast_in_dim.19.dom_ref, ...), custom_call_target="tpu_custom_call" | custom-call | flops 6442450944 | bytes 7340032 | tf_op jit(solution)/shard_map/transform/pallas_call | solution.py:86
  49.4 2.9 collective-permute-start.8
  57.8 14.8 %collective-permute-done.7 = bf16[256,512]{1,0:T(8,128)(2,1)S(1)} collective-permute-done((bf16[256,512]{1,0:T(8,128)(2,1)S(1)}, bf16[256,512]{1,0:T(8,128)(2,1)S(1)}, u32[]{:S(2)}, u32[]{:S(2)}) %collective-permute-start.7) | collective-permute-done | bytes 262176 | tf_op jit(solution)/shard_map/ppermute | solution.py:251
  75.3 4.4 %collective-permute-start = (bf16[256,512]{1,0:T(8,128)(2,1)S(1)}, bf16[256,512]{1,0:T(8,128)(2,1)S(1)}, u32[]{:S(2)}, u32[]{:S(2)}) collective-permute-start(bf16[256,512]{1,0:T(8,128)(2,1)S(1)} %get-tuple-element.38), channel_id=1, source_target_pairs={{0,8},{8,16},{16,24},{24,0},{1,9},{9,17},{17,25},{25,1},{2,10},{10... | collective-permute-start | bytes 786440 | tf_op jit(solution)/shard_map/ppermute | solution.py:251
  79.8 5.8 %collective-permute-start.1 = (bf16[256,512]{1,0:T(8,128)(2,1)S(1)}, bf16[256,512]{1,0:T(8,128)(2,1)S(1)}, u32[]{:S(2)}, u32[]{:S(2)}) collective-permute-start(bf16[256,512]{1,0:T(8,128)(2,1)S(1)} %get-tuple-element.39), channel_id=1, source_target_pairs={{0,16},{8,24},{16,0},{24,8},{1,17},{9,25},{17,1},{25,9},{2,18},{10... | collective-permute-start | bytes 786440 | tf_op jit(solution)/shard_map/ppermute | solution.py:251
  85.6 9.4 %collective-permute-done.4 = bf16[256,512]{1,0:T(8,128)(2,1)S(1)} collective-permute-done((bf16[256,512]{1,0:T(8,128)(2,1)S(1)}, bf16[256,512]{1,0:T(8,128)(2,1)S(1)}, u32[]{:S(2)}, u32[]{:S(2)}) %collective-permute-start.4) | collective-permute-done | bytes 262176 | tf_op jit(solution)/shard_map/ppermute | solution.py:251
  100.9 5.4 %collective-permute-done.1 = bf16[256,512]{1,0:T(8,128)(2,1)S(1)} collective-permute-done((bf16[256,512]{1,0:T(8,128)(2,1)S(1)}, bf16[256,512]{1,0:T(8,128)(2,1)S(1)}, u32[]{:S(2)}, u32[]{:S(2)}) %collective-permute-start.1) | collective-permute-done | bytes 262176 | tf_op jit(solution)/shard_map/ppermute | solution.py:251
  113.9 10.1 %collective-permute-done.18.refs_10_ = bf16[1024,512]{1,0:T(8,128)(2,1)S(1)} collective-permute-done((bf16[1024,512]{1,0:T(8,128)(2,1)S(1)}, bf16[1024,512]{1,0:T(8,128)(2,1)S(1)}, u32[]{:S(2)}, u32[]{:S(2)}) %collective-permute-start.18) | collective-permute-done | bytes 1048608 | tf_op jit(solution)/shard_map/ppermute | solution.py:276
  124.0 22.5 %collective-permute-done.17.refs_9_ = bf16[1024,512]{1,0:T(8,128)(2,1)S(1)} collective-permute-done((bf16[1024,512]{1,0:T(8,128)(2,1)S(1)}, bf16[1024,512]{1,0:T(8,128)(2,1)S(1)}, u32[]{:S(2)}, u32[]{:S(2)}) %collective-permute-start.17) | collective-permute-done | bytes 1048608 | tf_op jit(solution)/shard_map/ppermute | solution.py:276
  148.7 16.7 %collective-permute-done.16.refs_8_ = bf16[1024,512]{1,0:T(8,128)(2,1)S(1)} collective-permute-done((bf16[1024,512]{1,0:T(8,128)(2,1)S(1)}, bf16[1024,512]{1,0:T(8,128)(2,1)S(1)}, u32[]{:S(2)}, u32[]{:S(2)}) %collective-permute-start.16) | collective-permute-done | bytes 1048608 | tf_op jit(solution)/shard_map/ppermute | solution.py:276
  166.4 4.4 %collective-permute-start.25 = (bf16[1024,512]{1,0:T(8,128)(2,1)S(1)}, bf16[1024,512]{1,0:T(8,128)(2,1)}, u32[]{:S(2)}, u32[]{:S(2)}) collective-permute-start(bf16[1024,512]{1,0:T(8,128)(2,1)S(1)} %constant_dynamic-update-slice_fusion.8.refs_1_.own_ref), channel_id=1, source_target_pairs={{4,1},{6,3},{0,5},{2,7},{12,9},{14,11},{8,13},{10,15},{20,17},{22,... | collective-permute-start | bytes 3145736 | tf_op jit(solution)/shard_map/ppermute | solution.py:278
  172.8 45.5 %gather_fusion = f32[8192]{0:T(1024)S(1)} fusion(f32[2048]{0:T(1024)S(1)} %copy-done, s32[8192]{0:T(1024)S(1)} %broadcast_clamp_fusion), kind=kCustom, calls=%fused_computation | custom fusion | bytes 98304 | tf_op jit(solution)/shard_map/jit(_take)/gather | solution.py:263
  218.4 3.5 %collective-permute-start.24 = (bf16[1024,512]{1,0:T(8,128)(2,1)S(1)}, bf16[1024,512]{1,0:T(8,128)(2,1)}, u32[]{:S(2)}, u32[]{:S(2)}) collective-permute-start(bf16[1024,512]{1,0:T(8,128)(2,1)S(1)} %constant_dynamic-update-slice_fusion.own_ref.refs_0_), channel_id=1, source_target_pairs={{4,1},{6,3},{0,5},{2,7},{12,9},{14,11},{8,13},{10,15},{20,17},{22,... | collective-permute-start | bytes 3145736 | tf_op jit(solution)/shard_map/ppermute | solution.py:278
  226.7 6.6 %collective-permute-done.24.refs_16_ = bf16[1024,512]{1,0:T(8,128)(2,1)} collective-permute-done((bf16[1024,512]{1,0:T(8,128)(2,1)S(1)}, bf16[1024,512]{1,0:T(8,128)(2,1)}, u32[]{:S(2)}, u32[]{:S(2)}) %collective-permute-start.24) | collective-permute-done | bytes 1048608 | tf_op jit(solution)/shard_map/ppermute | solution.py:278
  241.6 6.5 %pairs.7 = (bf16[256,512]{1,0:T(8,128)(2,1)S(1)}, bf16[256,512]{1,0:T(8,128)(2,1)S(1)}, bf16[256,512]{1,0:T(8,128)(2,1)S(1)}, bf16[256,512]{1,0:T(8,128)(2,1)S(1)}) custom-call(s32[1]{0:T(128)} %bitcast.25.live_ref, s32[16]{0:T(128)S(1)} %bitcast.26, s32[1]{0:T(128)} %bitcast.3.odd_ref, f32[16]{0:T(128)S(1)} %pad_maximum_fusion.occ_ref, ...), custom_call_target="tpu_custom_call" | custom-call | flops 4294967296 | bytes 3145728 | tf_op jit(solution)/shard_map/pairs/pallas_call | solution.py:181
  248.2 8.9 %collective-permute-start.38 = (bf16[256,512]{1,0:T(8,128)(2,1)S(1)}, bf16[256,512]{1,0:T(8,128)(2,1)S(1)}, u32[]{:S(2)}, u32[]{:S(2)}) collective-permute-start(bf16[256,512]{1,0:T(8,128)(2,1)S(1)} %get-tuple-element.67), channel_id=1, source_target_pairs={{0,16},{8,24},{16,0},{24,8},{1,17},{9,25},{17,1},{25,9},{2,18},{10... | collective-permute-start | bytes 786440 | tf_op jit(solution)/shard_map/ppermute | solution.py:251
  259.0 8.0 %pairs.6 = (bf16[256,512]{1,0:T(8,128)(2,1)S(1)}, bf16[256,512]{1,0:T(8,128)(2,1)S(1)}, bf16[256,512]{1,0:T(8,128)(2,1)S(1)}, bf16[256,512]{1,0:T(8,128)(2,1)S(1)}) custom-call(s32[1]{0:T(128)} %bitcast.24.live_ref, s32[16]{0:T(128)S(1)} %bitcast.27, s32[1]{0:T(128)} %bitcast.3.odd_ref, f32[16]{0:T(128)S(1)} %pad_maximum_fusion.occ_ref, ...), custom_call_target="tpu_custom_call" | custom-call | flops 4294967296 | bytes 3145728 | tf_op jit(solution)/shard_map/pairs/pallas_call | solution.py:181
  268.2 3.8 %collective-permute-start.36 = (bf16[256,512]{1,0:T(8,128)(2,1)S(1)}, bf16[256,512]{1,0:T(8,128)(2,1)S(1)}, u32[]{:S(2)}, u32[]{:S(2)}) collective-permute-start(bf16[256,512]{1,0:T(8,128)(2,1)S(1)} %get-tuple-element.64), channel_id=1, source_target_pairs={{0,8},{8,16},{16,24},{24,0},{1,9},{9,17},{17,25},{25,1},{2,10},{10... | collective-permute-start | bytes 786440 | tf_op jit(solution)/shard_map/ppermute | solution.py:251
  272.0 6.7 %collective-permute-done.38.refs_14_ = bf16[256,512]{1,0:T(8,128)(2,1)S(1)} collective-permute-done((bf16[256,512]{1,0:T(8,128)(2,1)S(1)}, bf16[256,512]{1,0:T(8,128)(2,1)S(1)}, u32[]{:S(2)}, u32[]{:S(2)}) %collective-permute-start.38) | collective-permute-done | bytes 262176 | tf_op jit(solution)/shard_map/ppermute | solution.py:251
  278.7 7.3 %pairs.4 = (bf16[256,512]{1,0:T(8,128)(2,1)S(1)}, bf16[256,512]{1,0:T(8,128)(2,1)S(1)}, bf16[256,512]{1,0:T(8,128)(2,1)S(1)}, bf16[256,512]{1,0:T(8,128)(2,1)S(1)}) custom-call(s32[1]{0:T(128)} %bitcast.22.live_ref, s32[16]{0:T(128)S(1)} %bitcast.29, s32[1]{0:T(128)} %bitcast.3.odd_ref, f32[16]{0:T(128)S(1)} %pad_maximum_fusion.occ_ref, ...), custom_call_target="tpu_custom_call" | custom-call | flops 4294967296 | bytes 3145728 | tf_op jit(solution)/shard_map/pairs/pallas_call | solution.py:181
  286.0 4.8 %collective-permute-start.32 = (bf16[256,512]{1,0:T(8,128)(2,1)S(1)}, bf16[256,512]{1,0:T(8,128)(2,1)S(1)}, u32[]{:S(2)}, u32[]{:S(2)}) collective-permute-start(bf16[256,512]{1,0:T(8,128)(2,1)S(1)} %get-tuple-element.59), channel_id=1, source_target_pairs={{0,16},{8,24},{16,0},{24,8},{1,17},{9,25},{17,1},{25,9},{2,18},{10... | collective-permute-start | bytes 786440 | tf_op jit(solution)/shard_map/ppermute | solution.py:251
  290.9 10.8 %collective-permute-start.33 = (bf16[256,512]{1,0:T(8,128)(2,1)S(1)}, bf16[256,512]{1,0:T(8,128)(2,1)S(1)}, u32[]{:S(2)}, u32[]{:S(2)}) collective-permute-start(bf16[256,512]{1,0:T(8,128)(2,1)S(1)} %get-tuple-element.60), channel_id=1, source_target_pairs={{0,8},{8,16},{16,24},{24,0},{1,9},{9,17},{17,25},{25,1},{2,10},{10... | collective-permute-start | bytes 786440 | tf_op jit(solution)/shard_map/ppermute | solution.py:251
  301.7 5.2 %collective-permute-done.35.refs_10_ = bf16[256,512]{1,0:T(8,128)(2,1)S(1)} collective-permute-done((bf16[256,512]{1,0:T(8,128)(2,1)S(1)}, bf16[256,512]{1,0:T(8,128)(2,1)S(1)}, u32[]{:S(2)}, u32[]{:S(2)}) %collective-permute-start.35) | collective-permute-done | bytes 262176 | tf_op jit(solution)/shard_map/ppermute | solution.py:251
  308.9 4.0 %collective-permute-start.30 = (bf16[256,512]{1,0:T(8,128)(2,1)S(1)}, bf16[256,512]{1,0:T(8,128)(2,1)S(1)}, u32[]{:S(2)}, u32[]{:S(2)}) collective-permute-start(bf16[256,512]{1,0:T(8,128)(2,1)S(1)} %get-tuple-element.56), channel_id=1, source_target_pairs={{0,8},{8,16},{16,24},{24,0},{1,9},{9,17},{17,25},{25,1},{2,10},{10... | collective-permute-start | bytes 786440 | tf_op jit(solution)/shard_map/ppermute | solution.py:251
  312.9 21.9 %collective-permute-done.32.refs_6_ = bf16[256,512]{1,0:T(8,128)(2,1)S(1)} collective-permute-done((bf16[256,512]{1,0:T(8,128)(2,1)S(1)}, bf16[256,512]{1,0:T(8,128)(2,1)S(1)}, u32[]{:S(2)}, u32[]{:S(2)}) %collective-permute-start.32) | collective-permute-done | bytes 262176 | tf_op jit(solution)/shard_map/ppermute | solution.py:251
  334.8 11.2 %collective-permute-done.29.refs_2_ = bf16[256,512]{1,0:T(8,128)(2,1)S(1)} collective-permute-done((bf16[256,512]{1,0:T(8,128)(2,1)S(1)}, bf16[256,512]{1,0:T(8,128)(2,1)S(1)}, u32[]{:S(2)}, u32[]{:S(2)}) %collective-permute-start.29) | collective-permute-done | bytes 262176 | tf_op jit(solution)/shard_map/ppermute | solution.py:251
  346.0 3.3 assemble.1
  (139 shorter events, 51.3 us)
Async XLA Ops:
  16.1 33.3 %collective-permute-start.9 = (bf16[256,512]{1,0:T(8,128)(2,1)S(1)}, bf16[256,512]{1,0:T(8,128)(2,1)S(1)}, u32[]{:S(2)}, u32[]{:S(2)}) collective-permute-start(bf16[256,512]{1,0:T(8,128)(2,1)S(1)} %get-tuple-element.50), channel_id=1, source_target_pairs={{0,8},{8,16},{16,24},{24,0},{1,9},{9,17},{17,25},{25,1},{2,10},{10... | collective-permute-start | bytes 786440 | tf_op jit(solution)/shard_map/ppermute | solution.py:251
  19.2 33.1 %collective-permute-start.10 = (bf16[256,512]{1,0:T(8,128)(2,1)S(1)}, bf16[256,512]{1,0:T(8,128)(2,1)S(1)}, u32[]{:S(2)}, u32[]{:S(2)}) collective-permute-start(bf16[256,512]{1,0:T(8,128)(2,1)S(1)} %get-tuple-element.51), channel_id=1, source_target_pairs={{0,16},{8,24},{16,0},{24,8},{1,17},{9,25},{17,1},{25,9},{2,18},{10... | collective-permute-start | bytes 786440 | tf_op jit(solution)/shard_map/ppermute | solution.py:251
  21.8 31.2 %collective-permute-start.11 = (bf16[256,512]{1,0:T(8,128)(2,1)S(1)}, bf16[256,512]{1,0:T(8,128)(2,1)S(1)}, u32[]{:S(2)}, u32[]{:S(2)}) collective-permute-start(bf16[256,512]{1,0:T(8,128)(2,1)S(1)} %get-tuple-element.52), channel_id=1, source_target_pairs={{0,24},{8,0},{16,8},{24,16},{1,25},{9,1},{17,9},{25,17},{2,26},{10... | collective-permute-start | bytes 786440 | tf_op jit(solution)/shard_map/ppermute | solution.py:251
  32.2 40.4 %collective-permute-start.7 = (bf16[256,512]{1,0:T(8,128)(2,1)S(1)}, bf16[256,512]{1,0:T(8,128)(2,1)S(1)}, u32[]{:S(2)}, u32[]{:S(2)}) collective-permute-start(bf16[256,512]{1,0:T(8,128)(2,1)S(1)} %get-tuple-element.47), channel_id=1, source_target_pairs={{0,16},{8,24},{16,0},{24,8},{1,17},{9,25},{17,1},{25,9},{2,18},{10... | collective-permute-start | bytes 786440 | tf_op jit(solution)/shard_map/ppermute | solution.py:251
  49.4 25.9 %collective-permute-start.8 = (bf16[256,512]{1,0:T(8,128)(2,1)S(1)}, bf16[256,512]{1,0:T(8,128)(2,1)S(1)}, u32[]{:S(2)}, u32[]{:S(2)}) collective-permute-start(bf16[256,512]{1,0:T(8,128)(2,1)S(1)} %get-tuple-element.48), channel_id=1, source_target_pairs={{0,24},{8,0},{16,8},{24,16},{1,25},{9,1},{17,9},{25,17},{2,26},{10... | collective-permute-start | bytes 786440 | tf_op jit(solution)/shard_map/ppermute | solution.py:251
  52.3 27.5 %collective-permute-start.3 = (bf16[256,512]{1,0:T(8,128)(2,1)S(1)}, bf16[256,512]{1,0:T(8,128)(2,1)S(1)}, u32[]{:S(2)}, u32[]{:S(2)}) collective-permute-start(bf16[256,512]{1,0:T(8,128)(2,1)S(1)} %get-tuple-element.42), channel_id=1, source_target_pairs={{0,8},{8,16},{16,24},{24,0},{1,9},{9,17},{17,25},{25,1},{2,10},{10... | collective-permute-start | bytes 786440 | tf_op jit(solution)/shard_map/ppermute | solution.py:251
  52.9 42.1 %collective-permute-start.4 = (bf16[256,512]{1,0:T(8,128)(2,1)S(1)}, bf16[256,512]{1,0:T(8,128)(2,1)S(1)}, u32[]{:S(2)}, u32[]{:S(2)}) collective-permute-start(bf16[256,512]{1,0:T(8,128)(2,1)S(1)} %get-tuple-element.43), channel_id=1, source_target_pairs={{0,16},{8,24},{16,0},{24,8},{1,17},{9,25},{17,1},{25,9},{2,18},{10... | collective-permute-start | bytes 786440 | tf_op jit(solution)/shard_map/ppermute | solution.py:251
  55.3 56.0 %collective-permute-start.19 = (bf16[1024,512]{1,0:T(8,128)(2,1)S(1)}, bf16[1024,512]{1,0:T(8,128)(2,1)S(1)}, u32[]{:S(2)}, u32[]{:S(2)}) collective-permute-start(bf16[1024,512]{1,0:T(8,128)(2,1)S(1)} %constant_dynamic-update-slice_fusion.16.refs_3_.own_ref), channel_id=1, source_target_pairs={{0,6},{1,7},{2,0},{3,1},{4,2},{5,3},{6,4},{7,5},{8,14},{9,15},{10,... | collective-permute-start | bytes 3145736 | tf_op jit(solution)/shard_map/ppermute | solution.py:276
  72.6 25.2 %collective-permute-start.5 = (bf16[256,512]{1,0:T(8,128)(2,1)S(1)}, bf16[256,512]{1,0:T(8,128)(2,1)S(1)}, u32[]{:S(2)}, u32[]{:S(2)}) collective-permute-start(bf16[256,512]{1,0:T(8,128)(2,1)S(1)} %get-tuple-element.44), channel_id=1, source_target_pairs={{0,24},{8,0},{16,8},{24,16},{1,25},{9,1},{17,9},{25,17},{2,26},{10... | collective-permute-start | bytes 786440 | tf_op jit(solution)/shard_map/ppermute | solution.py:251
  75.3 25.0 %collective-permute-start = (bf16[256,512]{1,0:T(8,128)(2,1)S(1)}, bf16[256,512]{1,0:T(8,128)(2,1)S(1)}, u32[]{:S(2)}, u32[]{:S(2)}) collective-permute-start(bf16[256,512]{1,0:T(8,128)(2,1)S(1)} %get-tuple-element.38), channel_id=1, source_target_pairs={{0,8},{8,16},{16,24},{24,0},{1,9},{9,17},{17,25},{25,1},{2,10},{10... | collective-permute-start | bytes 786440 | tf_op jit(solution)/shard_map/ppermute | solution.py:251
  79.8 26.6 %collective-permute-start.1 = (bf16[256,512]{1,0:T(8,128)(2,1)S(1)}, bf16[256,512]{1,0:T(8,128)(2,1)S(1)}, u32[]{:S(2)}, u32[]{:S(2)}) collective-permute-start(bf16[256,512]{1,0:T(8,128)(2,1)S(1)} %get-tuple-element.39), channel_id=1, source_target_pairs={{0,16},{8,24},{16,0},{24,8},{1,17},{9,25},{17,1},{25,9},{2,18},{10... | collective-permute-start | bytes 786440 | tf_op jit(solution)/shard_map/ppermute | solution.py:251
  97.8 26.2 %collective-permute-start.18 = (bf16[1024,512]{1,0:T(8,128)(2,1)S(1)}, bf16[1024,512]{1,0:T(8,128)(2,1)S(1)}, u32[]{:S(2)}, u32[]{:S(2)}) collective-permute-start(bf16[1024,512]{1,0:T(8,128)(2,1)S(1)} %constant_dynamic-update-slice_fusion.12.refs_2_.own_ref), channel_id=1, source_target_pairs={{0,6},{1,7},{2,0},{3,1},{4,2},{5,3},{6,4},{7,5},{8,14},{9,15},{10,... | collective-permute-start | bytes 3145736 | tf_op jit(solution)/shard_map/ppermute | solution.py:276
  100.3 46.1 %collective-permute-start.17 = (bf16[1024,512]{1,0:T(8,128)(2,1)S(1)}, bf16[1024,512]{1,0:T(8,128)(2,1)S(1)}, u32[]{:S(2)}, u32[]{:S(2)}) collective-permute-start(bf16[1024,512]{1,0:T(8,128)(2,1)S(1)} %constant_dynamic-update-slice_fusion.8.refs_1_.own_ref), channel_id=1, source_target_pairs={{0,6},{1,7},{2,0},{3,1},{4,2},{5,3},{6,4},{7,5},{8,14},{9,15},{10,... | collective-permute-start | bytes 3145736 | tf_op jit(solution)/shard_map/ppermute | solution.py:276
  108.8 56.6 %collective-permute-start.16 = (bf16[1024,512]{1,0:T(8,128)(2,1)S(1)}, bf16[1024,512]{1,0:T(8,128)(2,1)S(1)}, u32[]{:S(2)}, u32[]{:S(2)}) collective-permute-start(bf16[1024,512]{1,0:T(8,128)(2,1)S(1)} %constant_dynamic-update-slice_fusion.own_ref.refs_0_), channel_id=1, source_target_pairs={{0,6},{1,7},{2,0},{3,1},{4,2},{5,3},{6,4},{7,5},{8,14},{9,15},{10,... | collective-permute-start | bytes 3145736 | tf_op jit(solution)/shard_map/ppermute | solution.py:276
  111.3 54.1 %collective-permute-start.15 = (bf16[1024,512]{1,0:T(8,128)(2,1)S(1)}, bf16[1024,512]{1,0:T(8,128)(2,1)S(1)}, u32[]{:S(2)}, u32[]{:S(2)}) collective-permute-start(bf16[1024,512]{1,0:T(8,128)(2,1)S(1)} %constant_dynamic-update-slice_fusion.16.refs_3_.own_ref), channel_id=1, source_target_pairs={{0,1},{1,0},{2,3},{3,2},{4,5},{5,4},{6,7},{7,6},{8,9},{9,8},{10,11... | collective-permute-start | bytes 3145736 | tf_op jit(solution)/shard_map/ppermute | solution.py:275
  111.3 59.6 %collective-permute-start.27 = (bf16[1024,512]{1,0:T(8,128)(2,1)S(1)}, bf16[1024,512]{1,0:T(8,128)(2,1)S(1)}, u32[]{:S(2)}, u32[]{:S(2)}) collective-permute-start(bf16[1024,512]{1,0:T(8,128)(2,1)S(1)} %constant_dynamic-update-slice_fusion.16.refs_3_.own_ref), channel_id=1, source_target_pairs={{4,1},{6,3},{0,5},{2,7},{12,9},{14,11},{8,13},{10,15},{20,17},{22,... | collective-permute-start | bytes 3145736 | tf_op jit(solution)/shard_map/ppermute | solution.py:278
  124.0 94.4 %collective-permute-start.14 = (bf16[1024,512]{1,0:T(8,128)(2,1)S(1)}, bf16[1024,512]{1,0:T(8,128)(2,1)}, u32[]{:S(2)}, u32[]{:S(2)}) collective-permute-start(bf16[1024,512]{1,0:T(8,128)(2,1)S(1)} %constant_dynamic-update-slice_fusion.12.refs_2_.own_ref), channel_id=1, source_target_pairs={{0,1},{1,0},{2,3},{3,2},{4,5},{5,4},{6,7},{7,6},{8,9},{9,8},{10,11... | collective-permute-start | bytes 3145736 | tf_op jit(solution)/shard_map/ppermute | solution.py:275
  146.4 75.5 %collective-permute-start.26 = (bf16[1024,512]{1,0:T(8,128)(2,1)S(1)}, bf16[1024,512]{1,0:T(8,128)(2,1)}, u32[]{:S(2)}, u32[]{:S(2)}) collective-permute-start(bf16[1024,512]{1,0:T(8,128)(2,1)S(1)} %constant_dynamic-update-slice_fusion.12.refs_2_.own_ref), channel_id=1, source_target_pairs={{4,1},{6,3},{0,5},{2,7},{12,9},{14,11},{8,13},{10,15},{20,17},{22,... | collective-permute-start | bytes 3145736 | tf_op jit(solution)/shard_map/ppermute | solution.py:278
  165.4 56.5 %collective-permute-start.13 = (bf16[1024,512]{1,0:T(8,128)(2,1)S(1)}, bf16[1024,512]{1,0:T(8,128)(2,1)}, u32[]{:S(2)}, u32[]{:S(2)}) collective-permute-start(bf16[1024,512]{1,0:T(8,128)(2,1)S(1)} %constant_dynamic-update-slice_fusion.8.refs_1_.own_ref), channel_id=1, source_target_pairs={{0,1},{1,0},{2,3},{3,2},{4,5},{5,4},{6,7},{7,6},{8,9},{9,8},{10,11... | collective-permute-start | bytes 3145736 | tf_op jit(solution)/shard_map/ppermute | solution.py:275
  166.4 56.0 %collective-permute-start.25 = (bf16[1024,512]{1,0:T(8,128)(2,1)S(1)}, bf16[1024,512]{1,0:T(8,128)(2,1)}, u32[]{:S(2)}, u32[]{:S(2)}) collective-permute-start(bf16[1024,512]{1,0:T(8,128)(2,1)S(1)} %constant_dynamic-update-slice_fusion.8.refs_1_.own_ref), channel_id=1, source_target_pairs={{4,1},{6,3},{0,5},{2,7},{12,9},{14,11},{8,13},{10,15},{20,17},{22,... | collective-permute-start | bytes 3145736 | tf_op jit(solution)/shard_map/ppermute | solution.py:278
  171.9 50.6 %collective-permute-start.12 = (bf16[1024,512]{1,0:T(8,128)(2,1)S(1)}, bf16[1024,512]{1,0:T(8,128)(2,1)}, u32[]{:S(2)}, u32[]{:S(2)}) collective-permute-start(bf16[1024,512]{1,0:T(8,128)(2,1)S(1)} %constant_dynamic-update-slice_fusion.own_ref.refs_0_), channel_id=1, source_target_pairs={{0,1},{1,0},{2,3},{3,2},{4,5},{5,4},{6,7},{7,6},{8,9},{9,8},{10,11... | collective-permute-start | bytes 3145736 | tf_op jit(solution)/shard_map/ppermute | solution.py:275
  248.2 30.5 %collective-permute-start.38 = (bf16[256,512]{1,0:T(8,128)(2,1)S(1)}, bf16[256,512]{1,0:T(8,128)(2,1)S(1)}, u32[]{:S(2)}, u32[]{:S(2)}) collective-permute-start(bf16[256,512]{1,0:T(8,128)(2,1)S(1)} %get-tuple-element.67), channel_id=1, source_target_pairs={{0,16},{8,24},{16,0},{24,8},{1,17},{9,25},{17,1},{25,9},{2,18},{10... | collective-permute-start | bytes 786440 | tf_op jit(solution)/shard_map/ppermute | solution.py:251
  257.0 29.0 %collective-permute-start.39 = (bf16[256,512]{1,0:T(8,128)(2,1)S(1)}, bf16[256,512]{1,0:T(8,128)(2,1)S(1)}, u32[]{:S(2)}, u32[]{:S(2)}) collective-permute-start(bf16[256,512]{1,0:T(8,128)(2,1)S(1)} %get-tuple-element.68), channel_id=1, source_target_pairs={{0,8},{8,16},{16,24},{24,0},{1,9},{9,17},{17,25},{25,1},{2,10},{10... | collective-permute-start | bytes 786440 | tf_op jit(solution)/shard_map/ppermute | solution.py:251
  267.0 23.9 %collective-permute-start.34 = (bf16[256,512]{1,0:T(8,128)(2,1)S(1)}, bf16[256,512]{1,0:T(8,128)(2,1)S(1)}, u32[]{:S(2)}, u32[]{:S(2)}) collective-permute-start(bf16[256,512]{1,0:T(8,128)(2,1)S(1)} %get-tuple-element.62), channel_id=1, source_target_pairs={{0,24},{8,0},{16,8},{24,16},{1,25},{9,1},{17,9},{25,17},{2,26},{10... | collective-permute-start | bytes 786440 | tf_op jit(solution)/shard_map/ppermute | solution.py:251
  267.0 39.8 %collective-permute-start.35 = (bf16[256,512]{1,0:T(8,128)(2,1)S(1)}, bf16[256,512]{1,0:T(8,128)(2,1)S(1)}, u32[]{:S(2)}, u32[]{:S(2)}) collective-permute-start(bf16[256,512]{1,0:T(8,128)(2,1)S(1)} %get-tuple-element.63), channel_id=1, source_target_pairs={{0,16},{8,24},{16,0},{24,8},{1,17},{9,25},{17,1},{25,9},{2,18},{10... | collective-permute-start | bytes 786440 | tf_op jit(solution)/shard_map/ppermute | solution.py:251
  268.2 38.6 %collective-permute-start.36 = (bf16[256,512]{1,0:T(8,128)(2,1)S(1)}, bf16[256,512]{1,0:T(8,128)(2,1)S(1)}, u32[]{:S(2)}, u32[]{:S(2)}) collective-permute-start(bf16[256,512]{1,0:T(8,128)(2,1)S(1)} %get-tuple-element.64), channel_id=1, source_target_pairs={{0,8},{8,16},{16,24},{24,0},{1,9},{9,17},{17,25},{25,1},{2,10},{10... | collective-permute-start | bytes 786440 | tf_op jit(solution)/shard_map/ppermute | solution.py:251
  278.7 30.3 %collective-permute-start.31 = (bf16[256,512]{1,0:T(8,128)(2,1)S(1)}, bf16[256,512]{1,0:T(8,128)(2,1)S(1)}, u32[]{:S(2)}, u32[]{:S(2)}) collective-permute-start(bf16[256,512]{1,0:T(8,128)(2,1)S(1)} %get-tuple-element.58), channel_id=1, source_target_pairs={{0,24},{8,0},{16,8},{24,16},{1,25},{9,1},{17,9},{25,17},{2,26},{10... | collective-permute-start | bytes 786440 | tf_op jit(solution)/shard_map/ppermute | solution.py:251
  286.0 48.8 %collective-permute-start.32 = (bf16[256,512]{1,0:T(8,128)(2,1)S(1)}, bf16[256,512]{1,0:T(8,128)(2,1)S(1)}, u32[]{:S(2)}, u32[]{:S(2)}) collective-permute-start(bf16[256,512]{1,0:T(8,128)(2,1)S(1)} %get-tuple-element.59), channel_id=1, source_target_pairs={{0,16},{8,24},{16,0},{24,8},{1,17},{9,25},{17,1},{25,9},{2,18},{10... | collective-permute-start | bytes 786440 | tf_op jit(solution)/shard_map/ppermute | solution.py:251
  290.9 43.9 %collective-permute-start.33 = (bf16[256,512]{1,0:T(8,128)(2,1)S(1)}, bf16[256,512]{1,0:T(8,128)(2,1)S(1)}, u32[]{:S(2)}, u32[]{:S(2)}) collective-permute-start(bf16[256,512]{1,0:T(8,128)(2,1)S(1)} %get-tuple-element.60), channel_id=1, source_target_pairs={{0,8},{8,16},{16,24},{24,0},{1,9},{9,17},{17,25},{25,1},{2,10},{10... | collective-permute-start | bytes 786440 | tf_op jit(solution)/shard_map/ppermute | solution.py:251
  306.8 28.0 %collective-permute-start.28 = (bf16[256,512]{1,0:T(8,128)(2,1)S(1)}, bf16[256,512]{1,0:T(8,128)(2,1)S(1)}, u32[]{:S(2)}, u32[]{:S(2)}) collective-permute-start(bf16[256,512]{1,0:T(8,128)(2,1)S(1)} %get-tuple-element.54), channel_id=1, source_target_pairs={{0,24},{8,0},{16,8},{24,16},{1,25},{9,1},{17,9},{25,17},{2,26},{10... | collective-permute-start | bytes 786440 | tf_op jit(solution)/shard_map/ppermute | solution.py:251
  306.8 39.2 %collective-permute-start.29 = (bf16[256,512]{1,0:T(8,128)(2,1)S(1)}, bf16[256,512]{1,0:T(8,128)(2,1)S(1)}, u32[]{:S(2)}, u32[]{:S(2)}) collective-permute-start(bf16[256,512]{1,0:T(8,128)(2,1)S(1)} %get-tuple-element.55), channel_id=1, source_target_pairs={{0,16},{8,24},{16,0},{24,8},{1,17},{9,25},{17,1},{25,9},{2,18},{10... | collective-permute-start | bytes 786440 | tf_op jit(solution)/shard_map/ppermute | solution.py:251
  308.9 37.1 %collective-permute-start.30 = (bf16[256,512]{1,0:T(8,128)(2,1)S(1)}, bf16[256,512]{1,0:T(8,128)(2,1)S(1)}, u32[]{:S(2)}, u32[]{:S(2)}) collective-permute-start(bf16[256,512]{1,0:T(8,128)(2,1)S(1)} %get-tuple-element.56), channel_id=1, source_target_pairs={{0,8},{8,16},{16,24},{24,0},{1,9},{9,17},{17,25},{25,1},{2,10},{10... | collective-permute-start | bytes 786440 | tf_op jit(solution)/shard_map/ppermute | solution.py:251
  (28 other events, 697.6 us)

commit v2 on v1

--- a/solution.py
+++ b/solution.py
@@ -54,7 +54,8 @@
     )(half_ints, mask)
 
 
-def transform_kernel(count, pos_ref, x_ref, dom_ref, coef_ref, *out_refs):
+def transform_kernel(count, after, pos_ref, x_ref, dom_ref, coef_ref, *refs):
+    out_refs = refs[after:]
     step = pl.program_id(0)
     tile = 512
     whole = coef_ref.shape[1]
@@ -75,16 +76,16 @@
             out_refs[index][...] = total
 
 
-def transformed(rows_of, own_domains, vir_coef, aux_pos, chunk, count):
+def transformed(rows_of, own_domains, vir_coef, aux_pos, aux_count, chunk, first, count, after):
     orbitals, rows, basis = rows_of.shape
     virs = own_domains.shape[2]
     whole = vir_coef.shape[1]
 
     def orbital(step, pos_ref):
-        return lax.rem(pos_ref[0] + step, count) * OCC_DEV + chunk
-
-    return pl.pallas_call(
-        functools.partial(transform_kernel, count),
+        return lax.rem(pos_ref[0] + first + step, aux_count) * OCC_DEV + chunk
+
+    return pl.pallas_call(
+        functools.partial(transform_kernel, count, len(after)),
         grid_spec=pltpu.PrefetchScalarGridSpec(
             num_scalar_prefetch=1,
             grid=(count,),
@@ -92,7 +93,8 @@
                 pl.BlockSpec((None, rows, basis), lambda g, pos: (orbital(g, pos), 0, 0)),
                 pl.BlockSpec((None, 1, virs), lambda g, pos: (orbital(g, pos), 0, 0)),
                 pl.BlockSpec((basis, whole), lambda g, pos: (0, 0), pipeline_mode=pl.Buffered(1)),
-            ],
+            ]
+            + [pl.BlockSpec(memory_space=pl.ANY)] * len(after),
             out_specs=[pl.BlockSpec((rows, virs), lambda g, pos: (0, 0)) for _ in range(count)],
         ),
         out_shape=[jax.ShapeDtypeStruct((rows, virs), jnp.bfloat16) for _ in range(count)],
@@ -103,14 +105,106 @@
             transcendentals=0,
         ),
         name="transform",
-    )(aux_pos, rows_of, own_domains, vir_coef)
+    )(aux_pos, rows_of, own_domains, vir_coef, *after)
+
+
+def join_kernel(count, after, flag_ref, *refs):
+    pieces, out, sems = refs[:count], refs[count + after], refs[count + after + 1]
+    rows = pieces[0].shape[0]
+    copies = [
+        pltpu.make_async_copy(piece, out.at[pl.ds(index * rows, rows)], sems.at[index])
+        for index, piece in enumerate(pieces)
+    ]
+    for copy in copies:
+        copy.start()
+    for copy in copies:
+        copy.wait()
+
+
+def pick_kernel(flag_ref, own_ref, near_ref, late_ref, *refs):
+    out, sems = refs[-2:]
+    rows = own_ref.shape[0]
+    first = pltpu.make_async_copy(own_ref, out.at[pl.ds(0, rows)], sems.at[0])
+    near = pltpu.make_async_copy(near_ref, out.at[pl.ds(rows, rows)], sems.at[1])
+    late = pltpu.make_async_copy(late_ref, out.at[pl.ds(rows, rows)], sems.at[1])
+    first.start()
+
+    @pl.when(flag_ref[0] == 0)
+    def _():
+        near.start()
+
+    @pl.when(flag_ref[0] != 0)
+    def _():
+        late.start()
+
+    first.wait()
+    near.wait()
+
+
+def stacked(pieces, flag, after):
+    rows = sum(piece.shape[0] for piece in pieces)
+    held = pl.BlockSpec(memory_space=pl.ANY)
+    return pl.pallas_call(
+        functools.partial(join_kernel, len(pieces), len(after)),
+        in_specs=[pl.BlockSpec(memory_space=pltpu.SMEM)] + [held] * (len(pieces) + len(after)),
+        out_specs=held,
+        out_shape=jax.ShapeDtypeStruct((rows,) + pieces[0].shape[1:], pieces[0].dtype),
+        scratch_shapes=[pltpu.SemaphoreType.DMA((len(pieces),))],
+        cost_estimate=pl.CostEstimate(
+            flops=0, bytes_accessed=4 * rows * pieces[0].shape[1], transcendentals=0
+        ),
+        name="join",
+    )(flag, *pieces, *after)
+
+
+def with_next(own, near, late, flag, after):
+    rows = own.shape[0]
+    held = pl.BlockSpec(memory_space=pl.ANY)
+    return pl.pallas_call(
+        pick_kernel,
+        in_specs=[pl.BlockSpec(memory_space=pltpu.SMEM)] + [held] * (3 + len(after)),
+        out_specs=held,
+        out_shape=jax.ShapeDtypeStruct((2 * rows,) + own.shape[1:], own.dtype),
+        scratch_shapes=[pltpu.SemaphoreType.DMA((2,))],
+        cost_estimate=pl.CostEstimate(flops=0, bytes_accessed=8 * rows * own.shape[1], transcendentals=0),
+        name="pick",
+    )(flag, own, near, late, *after)
+
+
+def energy_kernel(dom_ref, table_ref, row_ref, col_ref):
+    slots, virs = dom_ref.shape
+    lanes = table_ref.shape[1]
+    for part in range(virs // lanes):
+        span = slice(part * lanes, (part + 1) * lanes)
+        dom = dom_ref[:, span]
+        high, low = dom // lanes, dom % lanes
+        total = jnp.zeros((slots, lanes), jnp.float32)
+        for line in range(table_ref.shape[0]):
+            table = jnp.broadcast_to(table_ref[line : line + 1, :], (slots, lanes))
+            found = jnp.take_along_axis(table, low, axis=1, mode="promise_in_bounds")
+            total = jnp.where(high == line, found, total)
+        row_ref[:, 0, span] = total
+        col_ref[span, :] = total.T
+
+
+def energies(dom, vir_energy):
+    slots, virs = dom.shape
+    return pl.pallas_call(
+        energy_kernel,
+        out_shape=[
+            jax.ShapeDtypeStruct((slots, 1, virs), jnp.float32),
+            jax.ShapeDtypeStruct((virs, slots), jnp.float32),
+        ],
+        name="energies",
+    )(dom, vir_energy.reshape(-1, 128))
 
 
 def pair_kernel(chunk, count, live_ref, code_ref, odd_ref, occ_ref, own_ref, col_ref, row_ref, *refs):
-    kinds = 5
-    blocks = refs[: kinds * OCC_DEV]
-    outs = refs[kinds * OCC_DEV : kinds * OCC_DEV + count]
-    turned, total, held, sems, todo = refs[kinds * OCC_DEV + count :]
+    sets = 3
+    rows = own_ref.shape[0]
+    blocks = refs[: sets * OCC_DEV]
+    outs = refs[sets * OCC_DEV : sets * OCC_DEV + count]
+    turned, total, held, sems, todo = refs[sets * OCC_DEV + count :]
     span = PARTNERS * OCC_DEV
     slots = code_ref.shape[0]
     odd = odd_ref[0]
@@ -129,18 +223,21 @@
 
     def source(slot):
         offset = slot // OCC_DEV
-        one = jnp.where(odd == 1, 3, 1)
+        one = jnp.where(odd == 1, 3, 2)
         three = jnp.where(odd == 1, 4, 3)
-        kind = jnp.where(offset == 0, 0, jnp.where(offset == 1, one, jnp.where(offset == 2, 2, three)))
+        kind = jnp.where(offset == 0, 0, jnp.where(offset == 1, one, jnp.where(offset == 2, 1, three)))
         return kind * OCC_DEV + slot % OCC_DEV
 
     def fetch(index):
         place = source(todo[index])
         buffer = lax.rem(index, 2)
-        for number, block in enumerate(blocks):
-            @pl.when(place == number)
-            def _():
-                pltpu.make_async_copy(block, held.at[buffer], sems.at[buffer]).start()
+        for kind in range(5):
+            for orbital in range(OCC_DEV):
+                block = blocks[kind // 2 * OCC_DEV + orbital].at[pl.ds(kind % 2 * rows, rows)]
+
+                @pl.when(place == kind * OCC_DEV + orbital)
+                def _():
+                    pltpu.make_async_copy(block, held.at[buffer], sems.at[buffer]).start()
 
     @pl.when(pairs > 0)
     def _():
@@ -155,12 +252,12 @@
             fetch(index + 1)
 
         buffer = lax.rem(index, 2)
-        pltpu.make_async_copy(blocks[0], held.at[buffer], sems.at[buffer]).wait()
+        pltpu.make_async_copy(blocks[0].at[pl.ds(0, rows)], held.at[buffer], sems.at[buffer]).wait()
         slot = todo[index]
         shift = occ_ref[chunk] + occ_ref[slot]
         other = held[buffer]
         exchange = jnp.dot(turned[...], other, preferred_element_type=jnp.float32)
-        denom = (col_ref[...] + row_ref[slot]) - shift
+        denom = (col_ref[:, chunk : chunk + 1] + row_ref[slot]) - shift
         amplitude = (exchange / denom).astype(jnp.bfloat16)
         total[...] += lax.dot_general(
             other, amplitude, (((1,), (1,)), ((), ())), preferred_element_type=jnp.float32
@@ -168,9 +265,9 @@
         return carry
 
     lax.fori_loop(0, pairs, step, jnp.int32(0))
-    rows = outs[0].shape[0]
+    part = outs[0].shape[0]
     for index, out in enumerate(outs):
-        out[...] = total[index * rows : (index + 1) * rows, :].astype(jnp.bfloat16)
+        out[...] = total[index * part : (index + 1) * part, :].astype(jnp.bfloat16)
 
 
 def densities(chunk, count, live, codes, odd, partner_occ, own, own_vir, vir_rows, blocks):
@@ -181,7 +278,7 @@
     return pl.pallas_call(
         functools.partial(pair_kernel, chunk, count),
         in_specs=[smem, smem, smem, smem, whole(own.shape), whole(own_vir.shape), whole(vir_rows.shape)]
-        + [pl.BlockSpec(memory_space=pl.ANY)] * len(blocks),
+        + [pl.BlockSpec(memory_space=pltpu.HBM)] * len(blocks),
         out_specs=[whole((rows, virs))] * count,
         out_shape=[jax.ShapeDtypeStruct((rows, virs), jnp.bfloat16)] * count,
         scratch_shapes=[
@@ -260,33 +357,55 @@
         start = ((occ_pos + offset) % occ_count * aux_count + aux_pos) * OCC_DEV
         dom_rows.append(lax.dynamic_slice_in_dim(domains, start, OCC_DEV, 0))
         occ_rows.append(lax.dynamic_slice_in_dim(occ_energy, start, OCC_DEV, 0))
-    partner_vir = jnp.take(vir_energy, jnp.concatenate(dom_rows, axis=0))
+    vir_rows, vir_cols = energies(jnp.concatenate(dom_rows, axis=0), vir_energy)
     partner_occ = jnp.concatenate(occ_rows, axis=0)
 
-    twin = [(n, n ^ 1) for n in range(occ_count)]
-    next_chip = [(n, (n - 2) % occ_count) for n in range(occ_count)]
-    third = [((n + 3) % occ_count, n) for n in range(1, occ_count, 2)]
-    own, swap, chip, cross, far = [], [], [], [], []
+    twin, direct, far, last, late = routes(occ_count)
+    is_late = functools.reduce(jnp.logical_or, [occ_pos == n for n in late], jnp.bool_(False))
+    is_late = is_late.astype(jnp.int32).reshape(1)
+    owns, nears, sets, swaps, thirds = [], [], [], [], []
+    transform = functools.partial(transformed, rows_of, own_domains, vir_coef, pos, aux_count)
+    sent = [None] * aux_count
+    for step in list(range(1, aux_count)) + [0]:
+        sent[step] = transform(0, step, 1, [])[0]
+    after = [sent[0], vir_rows, partner_occ]
+    pieces = [sent[0]] + [along_aux(sent[step], step) for step in range(1, aux_count)]
     for chunk in range(OCC_DEV):
-        pieces = transformed(rows_of, own_domains, vir_coef, pos, chunk, aux_count)
-        pieces = [pieces[0]] + [along_aux(pieces[step], step) for step in range(1, aux_count)]
-        orbital = jnp.concatenate(pieces, axis=0)
-        own.append(orbital)
-        swap.append(lax.ppermute(orbital, "occ", twin))
-        chip.append(lax.ppermute(orbital, "occ", next_chip))
-        cross.append(lax.ppermute(chip[-1], "occ", twin))
-        far.append(lax.ppermute(orbital, "occ", third))
-    blocks = own + swap + chip + cross + far
+        coming = []
+        if chunk + 1 < OCC_DEV:
+            sent = transform(chunk + 1, 0, aux_count, after)
+            coming = [sent[0]] + [along_aux(sent[step], step) for step in range(1, aux_count)]
+        own = stacked(pieces, is_late, nears[-1:] + thirds[-1:] + swaps[-2:-1] + coming[:1])
+        near = lax.ppermute(own, "occ", direct)
+        third = lax.ppermute(own, "occ", far)
+        late_near = lax.ppermute(third, "occ", last) if last else near
+        both = with_next(own, near, late_near, is_late, coming[1:])
+        swap = lax.ppermute(both, "occ", twin)
+        for kind, value in zip((owns, nears, sets, swaps, thirds), (own, near, both, swap, third)):
+            kind.append(value)
+        pieces, after = coming, [own]
+    blocks = sets + swaps + thirds
     live = pair_count[0]
     codes = pair_code[0, 0]
     results = []
     for chunk in range(OCC_DEV):
         pieces = densities(
-            chunk, aux_count, live, codes, odd, partner_occ, own[chunk],
-            partner_vir[chunk][:, None], partner_vir[:, None, :], blocks,
+            chunk, aux_count, live, codes, odd, partner_occ, owns[chunk], vir_cols, vir_rows, blocks
         )
         results += [pieces[0]] + [along_aux(pieces[step], -step) for step in range(1, aux_count)]
     return assembled(results, pos, aux_count)
+
+
+def routes(count):
+    chips = count // 2
+    twin = [(n, n ^ 1) for n in range(count)]
+    turned = [c for c in range(0, chips, 2)] if chips == 4 else []
+    direct = [(n, (n - 2) % count) for n in range(count) if not (n % 2 and n // 2 in turned)]
+    far = [((n + 3) % count, n) for n in range(1, count, 2)]
+    far += [(2 * c + 1, 2 * ((c + 2) % chips)) for c in turned]
+    last = [(2 * ((c + 2) % chips), 2 * ((c - 1) % chips) + 1) for c in turned]
+    late = [target for _, target in last]
+    return twin, direct, far, last, late
 
 
 def solution(mesh):

time: 353 us -> 698 us (1.98)
  Pallas kernels: 65.7 us -> 467 us
  waiting for transfers between devices: 133 us -> 101 us
  local copies, waits for them, and re-layouts: 60.8 us -> 36.9 us
    pallas_call x4 -> x16, Pallas kernels: 33.4 us -> 427 us  [the longest x4 259 us: with_next(): pl.pallas_call(pick_kernel, in_specs=[pl.BlockSpec(memory_space=pltpu.SME...]
    gather x2 -> x0, local copies, waits for them, and re-layouts: 45.5 us -> none  [body(): partner_vir = jnp.take(vir_energy, jnp.concatenate(dom_rows, axis=0))]
    ppermute x16, waiting for transfers between devices: 55.8 us -> 24.4 us  [the longest x4 20.9 us: body(): third = lax.ppermute(own, 'occ', far)]
    unnamed x56 -> x106, local copies, waits for them, and re-layouts: 10.6 us -> 35 us
    ppermute x24, starting transfers between devices: 66.1 us -> 47.9 us  [along_aux(): lax.ppermute(value, 'aux', [(z, (z + steps) % aux_count) for z in range(a...]
    ppermute x16, starting transfers between devices: 21.9 us -> 39.5 us  [the longest x4 15.1 us: body(): late_near = lax.ppermute(third, 'occ', last) if last else near]
    pallas_call x4, Pallas kernels: 22.9 us -> 30.5 us  [densities(): pl.pallas_call(functools.partial(pair_kernel, chunk, count), in_specs=[sm...]
  transfers between devices with their start and end apart: 40 -> 40, of which waited for: 12 -> 14; matrix products, arithmetic and copies ran while one was open for 14% -> 0% of each run, Pallas kernels for 12% -> 55%
where the time goes in v2:
time: 698 us; the launch traced here: 696 us
  Pallas kernels  467 us (67%)
  waiting for transfers between devices  101 us (14%)
  starting transfers between devices  87.4 us (13%)
  local copies, waits for them, and re-layouts  36.9 us (5%)
    pallas_call x4, Pallas kernels, with_next(): pl.pallas_call(pick_kernel, in_specs=[pl.BlockSpec(memory_space=pltpu.SME...  259 us
    pallas_call x4, Pallas kernels, stacked(): pl.pallas_call(functools.partial(join_kernel, len(pieces), len(after)), i...  132 us
    ppermute x24, waiting for transfers between devices, along_aux(): lax.ppermute(value, 'aux', [(z, (z + steps) % aux_count) for z in range(a...  77 us
    ppermute x24, starting transfers between devices, along_aux(): lax.ppermute(value, 'aux', [(z, (z + steps) % aux_count) for z in range(a...  47.9 us
    pallas_call x7, Pallas kernels, transformed(): pl.pallas_call(functools.partial(transform_kernel, count, len(after)), gr...  35.1 us
    unnamed x106, local copies, waits for them, and re-layouts  35 us
    pallas_call x4, Pallas kernels, densities(): pl.pallas_call(functools.partial(pair_kernel, chunk, count), in_specs=[sm...  30.5 us
    ppermute x4, waiting for transfers between devices, body(): third = lax.ppermute(own, 'occ', far)  20.9 us
  transfers between devices with their start and end apart: 40, of which 14 were waited for; matrix products, arithmetic and copies ran while one was open for 0% of the time, Pallas kernels for 55%

profile of v2, /device:TPU:0, one launch (start us, length us, event | category | flops | bytes accessed | tf_op | source)
XLA Modules:
  0.0 695.5 jit_solution(17105662772279946842)
XLA Ops:
  1.6 6.1 sort_rows.1.x_ref
  38.5 8.3 %transform.11 = (bf16[256,512]{1,0:T(8,128)(2,1)S(1)}, bf16[256,512]{1,0:T(8,128)(2,1)S(1)}, bf16[256,512]{1,0:T(8,128)(2,1)S(1)}, bf16[256,512]{1,0:T(8,128)(2,1)S(1)}) custom-call(s32[1]{0:T(128)} %bitcast.pos_ref, bf16[16,256,1024]{2,1,0:T(8,128)(2,1)S(1)} %copy-done.2, s32[16,1,512]{2,1,0:T(1,128)S(1)} %broadcast_in_dim.7.dom_ref, ...), custom_call_target="tpu_custom_call" | custom-call | flops 6442450944 | bytes 7340032 | tf_op jit(solution)/shard_map/transform/pallas_call | solution.py:87
  48.4 32.9 %join.4.own_ref.refs_0_ = bf16[1024,512]{1,0:T(8,128)(2,1)} custom-call(s32[1]{0:T(128)} %bitcast.4.flag_ref, bf16[256,512]{1,0:T(8,128)(2,1)} %copy-done.27, bf16[256,512]{1,0:T(8,128)(2,1)} %copy-done.49, bf16[256,512]{1,0:T(8,128)(2,1)} %copy-done.50, bf16[256,512]{1,0:T(8,128)(2,1)} %copy-done.51, bf16[256,512]{1,0:T(8,128)(2,1)} %copy-done.28), custom_call_target="tpu_custom_call" | custom-call | bytes 2097152 | tf_op jit(solution)/shard_map/join/pallas_call | solution.py:147
  83.4 3.7 collective-permute-start.3
  94.4 9.4 %transform.12 = (bf16[256,512]{1,0:T(8,128)(2,1)S(1)}, bf16[256,512]{1,0:T(8,128)(2,1)S(1)}, bf16[256,512]{1,0:T(8,128)(2,1)S(1)}, bf16[256,512]{1,0:T(8,128)(2,1)S(1)}) custom-call(s32[1]{0:T(128)} %bitcast.pos_ref, bf16[16,256,1024]{2,1,0:T(8,128)(2,1)} %copy-done, s32[16,1,512]{2,1,0:T(1,128)S(1)} %broadcast_in_dim.7.dom_ref, ...), custom_call_target="tpu_custom_call" | custom-call | flops 6442450944 | bytes 7340032 | tf_op jit(solution)/shard_map/transform/pallas_call | solution.py:87
  114.0 32.9 %join.5.own_ref.refs_0_ = bf16[1024,512]{1,0:T(8,128)(2,1)} custom-call(s32[1]{0:T(128)} %bitcast.4.flag_ref, bf16[256,512]{1,0:T(8,128)(2,1)} %copy-done.28, bf16[256,512]{1,0:T(8,128)(2,1)} %copy-done.41, bf16[256,512]{1,0:T(8,128)(2,1)} %copy-done.43, bf16[256,512]{1,0:T(8,128)(2,1)} %copy-done.44, bf16[1024,512]{1,0:T(8,128)(2,1)} %copy-done.37, ...), custom_call_target="tpu_custom_call" | custom-call | bytes 2097152 | tf_op jit(solution)/shard_map/join/pallas_call | solution.py:147
  149.0 64.7 %pick.4.refs_0_ = bf16[2048,512]{1,0:T(8,128)(2,1)} custom-call(s32[1]{0:T(128)} %bitcast.4.flag_ref, bf16[1024,512]{1,0:T(8,128)(2,1)} %join.4.own_ref.refs_0_, bf16[1024,512]{1,0:T(8,128)(2,1)} %copy-done.37, bf16[1024,512]{1,0:T(8,128)(2,1)} %collective-permute-done.5.late_ref, bf16[256,512]{1,0:T(8,128)(2,1)} %copy-done.41, bf16[256,512]{1,0:T(8,128)(2,1)} %copy-done.43, ...), custom_call_target="tpu_custom_call" | custom-call | bytes 4194304 | tf_op jit(solution)/shard_map/pick/pallas_call | solution.py:163
  217.0 4.3 collective-permute-start.11
  222.6 10.0 %collective-permute-done.12.refs_0_.refs_1_ = bf16[256,512]{1,0:T(8,128)(2,1)S(1)} collective-permute-done((bf16[256,512]{1,0:T(8,128)(2,1)}, bf16[256,512]{1,0:T(8,128)(2,1)S(1)}, u32[]{:S(2)}, u32[]{:S(2)}) %collective-permute-start.12) | collective-permute-done | bytes 262176 | tf_op jit(solution)/shard_map/ppermute | solution.py:348
  233.4 6.3 collective-permute-done.13.refs_1_.refs_2_
  239.7 4.9 collective-permute-done.14.refs_2_.refs_3_
  246.3 64.6 %pick.5.refs_1_ = bf16[2048,512]{1,0:T(8,128)(2,1)} custom-call(s32[1]{0:T(128)} %bitcast.4.flag_ref, bf16[1024,512]{1,0:T(8,128)(2,1)} %join.5.own_ref.refs_0_, bf16[1024,512]{1,0:T(8,128)(2,1)} %copy-done.38, bf16[1024,512]{1,0:T(8,128)(2,1)} %collective-permute-done.11.late_ref, bf16[256,512]{1,0:T(8,128)(2,1)} %copy-done.46, ...), custom_call_target="tpu_custom_call" | custom-call | bytes 4194304 | tf_op jit(solution)/shard_map/pick/pallas_call | solution.py:163
  313.2 9.4 %transform.13 = (bf16[256,512]{1,0:T(8,128)(2,1)S(1)}, bf16[256,512]{1,0:T(8,128)(2,1)S(1)}, bf16[256,512]{1,0:T(8,128)(2,1)S(1)}, bf16[256,512]{1,0:T(8,128)(2,1)S(1)}) custom-call(s32[1]{0:T(128)} %bitcast.pos_ref, bf16[16,256,1024]{2,1,0:T(8,128)(2,1)} %copy-done, s32[16,1,512]{2,1,0:T(1,128)S(1)} %broadcast_in_dim.7.dom_ref, ...), custom_call_target="tpu_custom_call" | custom-call | flops 6442450944 | bytes 7340032 | tf_op jit(solution)/shard_map/transform/pallas_call | solution.py:87
  323.3 32.9 %join.6.own_ref = bf16[1024,512]{1,0:T(8,128)(2,1)} custom-call(s32[1]{0:T(128)} %bitcast.4.flag_ref, bf16[256,512]{1,0:T(8,128)(2,1)} %copy-done.29, bf16[256,512]{1,0:T(8,128)(2,1)} %copy-done.46, bf16[256,512]{1,0:T(8,128)(2,1)} %copy-done.47, bf16[256,512]{1,0:T(8,128)(2,1)} %copy-done.48, bf16[1024,512]{1,0:T(8,128)(2,1)} %copy-done.38, ...), custom_call_target="tpu_custom_call" | custom-call | bytes 2097152 | tf_op jit(solution)/shard_map/join/pallas_call | solution.py:147
  364.3 7.2 %collective-permute-done.19.refs_0_.refs_1_ = bf16[256,512]{1,0:T(8,128)(2,1)S(1)} collective-permute-done((bf16[256,512]{1,0:T(8,128)(2,1)S(1)}, bf16[256,512]{1,0:T(8,128)(2,1)S(1)}, u32[]{:S(2)}, u32[]{:S(2)}) %collective-permute-start.19) | collective-permute-done | bytes 262176 | tf_op jit(solution)/shard_map/ppermute | solution.py:348
  372.8 9.6 %collective-permute-done.20.refs_1_.refs_2_ = bf16[256,512]{1,0:T(8,128)(2,1)S(1)} collective-permute-done((bf16[256,512]{1,0:T(8,128)(2,1)S(1)}, bf16[256,512]{1,0:T(8,128)(2,1)S(1)}, u32[]{:S(2)}, u32[]{:S(2)}) %collective-permute-start.20) | collective-permute-done | bytes 262176 | tf_op jit(solution)/shard_map/ppermute | solution.py:348
  386.6 32.9 %join.7.own_ref = bf16[1024,512]{1,0:T(8,128)(2,1)} custom-call(s32[1]{0:T(128)} %bitcast.4.flag_ref, bf16[256,512]{1,0:T(8,128)(2,1)} %copy-done.30, bf16[256,512]{1,0:T(8,128)(2,1)} %copy-done.39, bf16[256,512]{1,0:T(8,128)(2,1)} %copy-done.40, bf16[256,512]{1,0:T(8,128)(2,1)} %copy-done.42, bf16[1024,512]{1,0:T(8,128)(2,1)} %copy-done.36, ...), custom_call_target="tpu_custom_call" | custom-call | bytes 2097152 | tf_op jit(solution)/shard_map/join/pallas_call | solution.py:147
  423.4 6.1 collective-permute-start.23
  429.5 17.4 %collective-permute-done.24.refs_11_ = bf16[1024,512]{1,0:T(8,128)(2,1)} collective-permute-done((bf16[1024,512]{1,0:T(8,128)(2,1)}, bf16[1024,512]{1,0:T(8,128)(2,1)}, u32[]{:S(2)}, u32[]{:S(2)}) %collective-permute-start.24) | collective-permute-done | bytes 1048608 | tf_op jit(solution)/shard_map/ppermute | solution.py:380
  446.9 6.1 collective-permute-start.25
  454.0 64.6 %pick.6.refs_2_ = bf16[2048,512]{1,0:T(8,128)(2,1)} custom-call(s32[1]{0:T(128)} %bitcast.4.flag_ref, bf16[1024,512]{1,0:T(8,128)(2,1)} %join.6.own_ref, bf16[1024,512]{1,0:T(8,128)(2,1)} %copy-done.36, bf16[1024,512]{1,0:T(8,128)(2,1)} %copy-done.45, bf16[256,512]{1,0:T(8,128)(2,1)} %copy-done.39, bf16[256,512]{1,0:T(8,128)(2,1)} %copy-done.40, ...), custom_call_target="tpu_custom_call" | custom-call | bytes 4194304 | tf_op jit(solution)/shard_map/pick/pallas_call | solution.py:163
  518.8 64.7 %pick.7.refs_3_ = bf16[2048,512]{1,0:T(8,128)(2,1)} custom-call(s32[1]{0:T(128)} %bitcast.4.flag_ref, bf16[1024,512]{1,0:T(8,128)(2,1)} %join.7.own_ref, bf16[1024,512]{1,0:T(8,128)(2,1)} %collective-permute-done.23.near_ref, bf16[1024,512]{1,0:T(8,128)(2,1)} %collective-permute-done.25.late_ref), custom_call_target="tpu_custom_call" | custom-call | bytes 4194304 | tf_op jit(solution)/shard_map/pick/pallas_call | solution.py:163
  595.0 5.8 pairs.7
  606.0 9.4 %pairs.6 = (bf16[256,512]{1,0:T(8,128)(2,1)S(1)}, bf16[256,512]{1,0:T(8,128)(2,1)S(1)}, bf16[256,512]{1,0:T(8,128)(2,1)S(1)}, bf16[256,512]{1,0:T(8,128)(2,1)S(1)}) custom-call(s32[1]{0:T(128)} %bitcast.9.live_ref, s32[16]{0:T(128)S(1)} %bitcast.12, s32[1]{0:T(128)} %bitcast.3.odd_ref, f32[16]{0:T(128)S(1)} %pad_maximum_fusion.refs_2_.occ_ref, ...), custom_call_target="tpu_custom_call" | custom-call | flops 4294967296 | bytes 3145728 | tf_op jit(solution)/shard_map/pairs/pallas_call | solution.py:278
  615.5 5.0 pairs.5
  622.5 15.2 %collective-permute-done.38.refs_14_ = bf16[256,512]{1,0:T(8,128)(2,1)S(1)} collective-permute-done((bf16[256,512]{1,0:T(8,128)(2,1)S(1)}, bf16[256,512]{1,0:T(8,128)(2,1)S(1)}, u32[]{:S(2)}, u32[]{:S(2)}) %collective-permute-start.38) | collective-permute-done | bytes 262176 | tf_op jit(solution)/shard_map/ppermute | solution.py:348
  637.7 10.3 %pairs.4 = (bf16[256,512]{1,0:T(8,128)(2,1)S(1)}, bf16[256,512]{1,0:T(8,128)(2,1)S(1)}, bf16[256,512]{1,0:T(8,128)(2,1)S(1)}, bf16[256,512]{1,0:T(8,128)(2,1)S(1)}) custom-call(s32[1]{0:T(128)} %bitcast.7.live_ref, s32[16]{0:T(128)S(1)} %bitcast.14, s32[1]{0:T(128)} %bitcast.3.odd_ref, f32[16]{0:T(128)S(1)} %pad_maximum_fusion.refs_2_.occ_ref, ...), custom_call_target="tpu_custom_call" | custom-call | flops 4294967296 | bytes 3145728 | tf_op jit(solution)/shard_map/pairs/pallas_call | solution.py:278
  648.1 5.7 collective-permute-start.33
  653.8 7.9 %collective-permute-done.35.refs_10_ = bf16[256,512]{1,0:T(8,128)(2,1)S(1)} collective-permute-done((bf16[256,512]{1,0:T(8,128)(2,1)S(1)}, bf16[256,512]{1,0:T(8,128)(2,1)S(1)}, u32[]{:S(2)}, u32[]{:S(2)}) %collective-permute-start.35) | collective-permute-done | bytes 262176 | tf_op jit(solution)/shard_map/ppermute | solution.py:348
  664.6 14.4 %collective-permute-start.30 = (bf16[256,512]{1,0:T(8,128)(2,1)S(1)}, bf16[256,512]{1,0:T(8,128)(2,1)S(1)}, u32[]{:S(2)}, u32[]{:S(2)}) collective-permute-start(bf16[256,512]{1,0:T(8,128)(2,1)S(1)} %get-tuple-element.52), channel_id=1, source_target_pairs={{0,8},{8,16},{16,24},{24,0},{1,9},{9,17},{17,25},{25,1},{2,10},{10... | collective-permute-start | bytes 786440 | tf_op jit(solution)/shard_map/ppermute | solution.py:348
  679.1 5.1 collective-permute-done.32.refs_6_
  684.1 8.1 %collective-permute-done.29.refs_2_ = bf16[256,512]{1,0:T(8,128)(2,1)S(1)} collective-permute-done((bf16[256,512]{1,0:T(8,128)(2,1)S(1)}, bf16[256,512]{1,0:T(8,128)(2,1)S(1)}, u32[]{:S(2)}, u32[]{:S(2)}) %collective-permute-start.29) | collective-permute-done | bytes 262176 | tf_op jit(solution)/shard_map/ppermute | solution.py:348
  (186 shorter events, 108.4 us)
Async XLA Ops:
  9.8 37.8 %collective-permute-start = (bf16[256,512]{1,0:T(8,128)(2,1)S(1)}, bf16[256,512]{1,0:T(8,128)(2,1)S(1)}, u32[]{:S(2)}, u32[]{:S(2)}) collective-permute-start(bf16[256,512]{1,0:T(8,128)(2,1)S(1)} %transform.8), channel_id=1, source_target_pairs={{0,8},{8,16},{16,24},{24,0},{1,9},{9,17},{17,25},{25,1},{2,10},{10... | collective-permute-start | bytes 786440 | tf_op jit(solution)/shard_map/ppermute | solution.py:348
  14.9 32.7 %collective-permute-start.1 = (bf16[256,512]{1,0:T(8,128)(2,1)S(1)}, bf16[256,512]{1,0:T(8,128)(2,1)S(1)}, u32[]{:S(2)}, u32[]{:S(2)}) collective-permute-start(bf16[256,512]{1,0:T(8,128)(2,1)S(1)} %transform.9), channel_id=1, source_target_pairs={{0,16},{8,24},{16,0},{24,8},{1,17},{9,25},{17,1},{25,9},{2,18},{10... | collective-permute-start | bytes 786440 | tf_op jit(solution)/shard_map/ppermute | solution.py:348
  19.6 28.0 %collective-permute-start.2 = (bf16[256,512]{1,0:T(8,128)(2,1)S(1)}, bf16[256,512]{1,0:T(8,128)(2,1)S(1)}, u32[]{:S(2)}, u32[]{:S(2)}) collective-permute-start(bf16[256,512]{1,0:T(8,128)(2,1)S(1)} %transform.10), channel_id=1, source_target_pairs={{0,24},{8,0},{16,8},{24,16},{1,25},{9,1},{17,9},{25,17},{2,26},{10... | collective-permute-start | bytes 786440 | tf_op jit(solution)/shard_map/ppermute | solution.py:348
  81.3 27.5 %collective-permute-start.4 = (bf16[1024,512]{1,0:T(8,128)(2,1)}, bf16[1024,512]{1,0:T(8,128)(2,1)S(1)}, u32[]{:S(2)}, u32[]{:S(2)}) collective-permute-start(bf16[1024,512]{1,0:T(8,128)(2,1)} %join.4.own_ref.refs_0_), channel_id=1, source_target_pairs={{4,1},{6,3},{0,5},{2,7},{1,4},{5,0},{12,9},{14,11},{8,13},{10,15},... | collective-permute-start | bytes 3145736 | tf_op jit(solution)/shard_map/ppermute | solution.py:380
  83.4 28.8 %collective-permute-start.3 = (bf16[1024,512]{1,0:T(8,128)(2,1)}, bf16[1024,512]{1,0:T(8,128)(2,1)S(1)}, u32[]{:S(2)}, u32[]{:S(2)}) collective-permute-start(bf16[1024,512]{1,0:T(8,128)(2,1)} %join.4.own_ref.refs_0_), channel_id=1, source_target_pairs={{0,6},{2,0},{3,1},{4,2},{6,4},{7,5},{8,14},{10,8},{11,9},{12,10},{... | collective-permute-start | bytes 3145736 | tf_op jit(solution)/shard_map/ppermute | solution.py:379
  87.1 25.1 %collective-permute-start.6 = (bf16[256,512]{1,0:T(8,128)(2,1)S(1)}, bf16[256,512]{1,0:T(8,128)(2,1)S(1)}, u32[]{:S(2)}, u32[]{:S(2)}) collective-permute-start(bf16[256,512]{1,0:T(8,128)(2,1)S(1)} %get-tuple-element.38), channel_id=1, source_target_pairs={{0,8},{8,16},{16,24},{24,0},{1,9},{9,17},{17,25},{25,1},{2,10},{10... | collective-permute-start | bytes 786440 | tf_op jit(solution)/shard_map/ppermute | solution.py:348
  87.8 24.4 %collective-permute-start.7 = (bf16[256,512]{1,0:T(8,128)(2,1)S(1)}, bf16[256,512]{1,0:T(8,128)(2,1)S(1)}, u32[]{:S(2)}, u32[]{:S(2)}) collective-permute-start(bf16[256,512]{1,0:T(8,128)(2,1)S(1)} %get-tuple-element.39), channel_id=1, source_target_pairs={{0,16},{8,24},{16,0},{24,8},{1,17},{9,25},{17,1},{25,9},{2,18},{10... | collective-permute-start | bytes 786440 | tf_op jit(solution)/shard_map/ppermute | solution.py:348
  88.1 24.0 %collective-permute-start.8 = (bf16[256,512]{1,0:T(8,128)(2,1)S(1)}, bf16[256,512]{1,0:T(8,128)(2,1)S(1)}, u32[]{:S(2)}, u32[]{:S(2)}) collective-permute-start(bf16[256,512]{1,0:T(8,128)(2,1)S(1)} %get-tuple-element.40), channel_id=1, source_target_pairs={{0,24},{8,0},{16,8},{24,16},{1,25},{9,1},{17,9},{25,17},{2,26},{10... | collective-permute-start | bytes 786440 | tf_op jit(solution)/shard_map/ppermute | solution.py:348
  108.8 40.2 %collective-permute-start.5 = (bf16[1024,512]{1,0:T(8,128)(2,1)S(1)}, bf16[1024,512]{1,0:T(8,128)(2,1)}, u32[]{:S(2)}, u32[]{:S(2)}) collective-permute-start(bf16[1024,512]{1,0:T(8,128)(2,1)S(1)} %collective-permute-done.4.refs_5_.refs_8_), channel_id=1, source_target_pairs={{4,7},{0,3},{12,15},{8,11},{20,23},{16,19},{28,31},{24,27}} | collective-permute-start | bytes 3145736 | tf_op jit(solution)/shard_map/ppermute | solution.py:381
  146.9 70.1 %collective-permute-start.10 = (bf16[1024,512]{1,0:T(8,128)(2,1)}, bf16[1024,512]{1,0:T(8,128)(2,1)S(1)}, u32[]{:S(2)}, u32[]{:S(2)}) collective-permute-start(bf16[1024,512]{1,0:T(8,128)(2,1)} %join.5.own_ref.refs_0_), channel_id=1, source_target_pairs={{4,1},{6,3},{0,5},{2,7},{1,4},{5,0},{12,9},{14,11},{8,13},{10,15},... | collective-permute-start | bytes 3145736 | tf_op jit(solution)/shard_map/ppermute | solution.py:380
  213.7 109.7 %collective-permute-start.15 = (bf16[2048,512]{1,0:T(8,128)(2,1)}, bf16[2048,512]{1,0:T(8,128)(2,1)}, u32[]{:S(2)}, u32[]{:S(2)}) collective-permute-start(bf16[2048,512]{1,0:T(8,128)(2,1)} %pick.4.refs_0_), channel_id=1, source_target_pairs={{0,1},{1,0},{2,3},{3,2},{4,5},{5,4},{6,7},{7,6},{8,9},{9,8},{10,11... | collective-permute-start | bytes 6291464 | tf_op jit(solution)/shard_map/ppermute | solution.py:383
  215.1 29.5 %collective-permute-start.9 = (bf16[1024,512]{1,0:T(8,128)(2,1)S(1)}, bf16[1024,512]{1,0:T(8,128)(2,1)S(1)}, u32[]{:S(2)}, u32[]{:S(2)}) collective-permute-start(bf16[1024,512]{1,0:T(8,128)(2,1)S(1)} %copy-done.21), channel_id=1, source_target_pairs={{0,6},{2,0},{3,1},{4,2},{6,4},{7,5},{8,14},{10,8},{11,9},{12,10},{... | collective-permute-start | bytes 3145736 | tf_op jit(solution)/shard_map/ppermute | solution.py:379
  217.0 29.3 %collective-permute-start.11 = (bf16[1024,512]{1,0:T(8,128)(2,1)S(1)}, bf16[1024,512]{1,0:T(8,128)(2,1)}, u32[]{:S(2)}, u32[]{:S(2)}) collective-permute-start(bf16[1024,512]{1,0:T(8,128)(2,1)S(1)} %collective-permute-done.10.refs_5_.refs_9_), channel_id=1, source_target_pairs={{4,7},{0,3},{12,15},{8,11},{20,23},{16,19},{28,31},{24,27}} | collective-permute-start | bytes 3145736 | tf_op jit(solution)/shard_map/ppermute | solution.py:381
  311.0 74.7 %collective-permute-start.22 = (bf16[2048,512]{1,0:T(8,128)(2,1)}, bf16[2048,512]{1,0:T(8,128)(2,1)}, u32[]{:S(2)}, u32[]{:S(2)}) collective-permute-start(bf16[2048,512]{1,0:T(8,128)(2,1)} %pick.5.refs_1_), channel_id=1, source_target_pairs={{0,1},{1,0},{2,3},{3,2},{4,5},{5,4},{6,7},{7,6},{8,9},{9,8},{10,11... | collective-permute-start | bytes 6291464 | tf_op jit(solution)/shard_map/ppermute | solution.py:383
  356.2 28.9 %collective-permute-start.16 = (bf16[1024,512]{1,0:T(8,128)(2,1)}, bf16[1024,512]{1,0:T(8,128)(2,1)S(1)}, u32[]{:S(2)}, u32[]{:S(2)}) collective-permute-start(bf16[1024,512]{1,0:T(8,128)(2,1)} %join.6.own_ref), channel_id=1, source_target_pairs={{0,6},{2,0},{3,1},{4,2},{6,4},{7,5},{8,14},{10,8},{11,9},{12,10},{... | collective-permute-start | bytes 3145736 | tf_op jit(solution)/shard_map/ppermute | solution.py:379
  358.2 27.5 %collective-permute-start.17 = (bf16[1024,512]{1,0:T(8,128)(2,1)}, bf16[1024,512]{1,0:T(8,128)(2,1)S(1)}, u32[]{:S(2)}, u32[]{:S(2)}) collective-permute-start(bf16[1024,512]{1,0:T(8,128)(2,1)} %join.6.own_ref), channel_id=1, source_target_pairs={{4,1},{6,3},{0,5},{2,7},{1,4},{5,0},{12,9},{14,11},{8,13},{10,15},... | collective-permute-start | bytes 3145736 | tf_op jit(solution)/shard_map/ppermute | solution.py:380
  419.6 27.4 %collective-permute-start.24 = (bf16[1024,512]{1,0:T(8,128)(2,1)}, bf16[1024,512]{1,0:T(8,128)(2,1)}, u32[]{:S(2)}, u32[]{:S(2)}) collective-permute-start(bf16[1024,512]{1,0:T(8,128)(2,1)} %join.7.own_ref), channel_id=1, source_target_pairs={{4,1},{6,3},{0,5},{2,7},{1,4},{5,0},{12,9},{14,11},{8,13},{10,15},... | collective-permute-start | bytes 3145736 | tf_op jit(solution)/shard_map/ppermute | solution.py:380
  422.0 31.0 %collective-permute-start.18 = (bf16[1024,512]{1,0:T(8,128)(2,1)}, bf16[1024,512]{1,0:T(8,128)(2,1)S(1)}, u32[]{:S(2)}, u32[]{:S(2)}) collective-permute-start(bf16[1024,512]{1,0:T(8,128)(2,1)} %copy-done.13), channel_id=1, source_target_pairs={{4,7},{0,3},{12,15},{8,11},{20,23},{16,19},{28,31},{24,27}} | collective-permute-start | bytes 3145736 | tf_op jit(solution)/shard_map/ppermute | solution.py:381
  423.4 95.4 %collective-permute-start.23 = (bf16[1024,512]{1,0:T(8,128)(2,1)}, bf16[1024,512]{1,0:T(8,128)(2,1)}, u32[]{:S(2)}, u32[]{:S(2)}) collective-permute-start(bf16[1024,512]{1,0:T(8,128)(2,1)} %join.7.own_ref), channel_id=1, source_target_pairs={{0,6},{2,0},{3,1},{4,2},{6,4},{7,5},{8,14},{10,8},{11,9},{12,10},{... | collective-permute-start | bytes 3145736 | tf_op jit(solution)/shard_map/ppermute | solution.py:379
  446.9 71.8 %collective-permute-start.25 = (bf16[1024,512]{1,0:T(8,128)(2,1)}, bf16[1024,512]{1,0:T(8,128)(2,1)}, u32[]{:S(2)}, u32[]{:S(2)}) collective-permute-start(bf16[1024,512]{1,0:T(8,128)(2,1)} %collective-permute-done.24.refs_11_), channel_id=1, source_target_pairs={{4,7},{0,3},{12,15},{8,11},{20,23},{16,19},{28,31},{24,27}} | collective-permute-start | bytes 3145736 | tf_op jit(solution)/shard_map/ppermute | solution.py:381
  518.7 66.0 %collective-permute-start.26 = (bf16[2048,512]{1,0:T(8,128)(2,1)}, bf16[2048,512]{1,0:T(8,128)(2,1)}, u32[]{:S(2)}, u32[]{:S(2)}) collective-permute-start(bf16[2048,512]{1,0:T(8,128)(2,1)} %pick.6.refs_2_), channel_id=1, source_target_pairs={{0,1},{1,0},{2,3},{3,2},{4,5},{5,4},{6,7},{7,6},{8,9},{9,8},{10,11... | collective-permute-start | bytes 6291464 | tf_op jit(solution)/shard_map/ppermute | solution.py:383
  600.9 36.8 %collective-permute-start.38 = (bf16[256,512]{1,0:T(8,128)(2,1)S(1)}, bf16[256,512]{1,0:T(8,128)(2,1)S(1)}, u32[]{:S(2)}, u32[]{:S(2)}) collective-permute-start(bf16[256,512]{1,0:T(8,128)(2,1)S(1)} %get-tuple-element.63), channel_id=1, source_target_pairs={{0,16},{8,24},{16,0},{24,8},{1,17},{9,25},{17,1},{25,9},{2,18},{10... | collective-permute-start | bytes 786440 | tf_op jit(solution)/shard_map/ppermute | solution.py:348
  604.0 44.0 %collective-permute-start.39 = (bf16[256,512]{1,0:T(8,128)(2,1)S(1)}, bf16[256,512]{1,0:T(8,128)(2,1)S(1)}, u32[]{:S(2)}, u32[]{:S(2)}) collective-permute-start(bf16[256,512]{1,0:T(8,128)(2,1)S(1)} %get-tuple-element.64), channel_id=1, source_target_pairs={{0,8},{8,16},{16,24},{24,0},{1,9},{9,17},{17,25},{25,1},{2,10},{10... | collective-permute-start | bytes 786440 | tf_op jit(solution)/shard_map/ppermute | solution.py:348
  615.3 32.8 %collective-permute-start.34 = (bf16[256,512]{1,0:T(8,128)(2,1)S(1)}, bf16[256,512]{1,0:T(8,128)(2,1)S(1)}, u32[]{:S(2)}, u32[]{:S(2)}) collective-permute-start(bf16[256,512]{1,0:T(8,128)(2,1)S(1)} %get-tuple-element.58), channel_id=1, source_target_pairs={{0,24},{8,0},{16,8},{24,16},{1,25},{9,1},{17,9},{25,17},{2,26},{10... | collective-permute-start | bytes 786440 | tf_op jit(solution)/shard_map/ppermute | solution.py:348
  615.4 46.3 %collective-permute-start.35 = (bf16[256,512]{1,0:T(8,128)(2,1)S(1)}, bf16[256,512]{1,0:T(8,128)(2,1)S(1)}, u32[]{:S(2)}, u32[]{:S(2)}) collective-permute-start(bf16[256,512]{1,0:T(8,128)(2,1)S(1)} %get-tuple-element.59), channel_id=1, source_target_pairs={{0,16},{8,24},{16,0},{24,8},{1,17},{9,25},{17,1},{25,9},{2,18},{10... | collective-permute-start | bytes 786440 | tf_op jit(solution)/shard_map/ppermute | solution.py:348
  620.5 41.2 %collective-permute-start.36 = (bf16[256,512]{1,0:T(8,128)(2,1)S(1)}, bf16[256,512]{1,0:T(8,128)(2,1)S(1)}, u32[]{:S(2)}, u32[]{:S(2)}) collective-permute-start(bf16[256,512]{1,0:T(8,128)(2,1)S(1)} %get-tuple-element.60), channel_id=1, source_target_pairs={{0,8},{8,16},{16,24},{24,0},{1,9},{9,17},{17,25},{25,1},{2,10},{10... | collective-permute-start | bytes 786440 | tf_op jit(solution)/shard_map/ppermute | solution.py:348
  637.7 27.0 %collective-permute-start.31 = (bf16[256,512]{1,0:T(8,128)(2,1)S(1)}, bf16[256,512]{1,0:T(8,128)(2,1)S(1)}, u32[]{:S(2)}, u32[]{:S(2)}) collective-permute-start(bf16[256,512]{1,0:T(8,128)(2,1)S(1)} %get-tuple-element.54), channel_id=1, source_target_pairs={{0,24},{8,0},{16,8},{24,16},{1,25},{9,1},{17,9},{25,17},{2,26},{10... | collective-permute-start | bytes 786440 | tf_op jit(solution)/shard_map/ppermute | solution.py:348
  648.0 36.1 %collective-permute-start.32 = (bf16[256,512]{1,0:T(8,128)(2,1)S(1)}, bf16[256,512]{1,0:T(8,128)(2,1)S(1)}, u32[]{:S(2)}, u32[]{:S(2)}) collective-permute-start(bf16[256,512]{1,0:T(8,128)(2,1)S(1)} %get-tuple-element.55), channel_id=1, source_target_pairs={{0,16},{8,24},{16,0},{24,8},{1,17},{9,25},{17,1},{25,9},{2,18},{10... | collective-permute-start | bytes 786440 | tf_op jit(solution)/shard_map/ppermute | solution.py:348
  648.1 36.0 %collective-permute-start.33 = (bf16[256,512]{1,0:T(8,128)(2,1)S(1)}, bf16[256,512]{1,0:T(8,128)(2,1)S(1)}, u32[]{:S(2)}, u32[]{:S(2)}) collective-permute-start(bf16[256,512]{1,0:T(8,128)(2,1)S(1)} %get-tuple-element.56), channel_id=1, source_target_pairs={{0,8},{8,16},{16,24},{24,0},{1,9},{9,17},{17,25},{25,1},{2,10},{10... | collective-permute-start | bytes 786440 | tf_op jit(solution)/shard_map/ppermute | solution.py:348
  661.7 22.4 %collective-permute-start.28 = (bf16[256,512]{1,0:T(8,128)(2,1)S(1)}, bf16[256,512]{1,0:T(8,128)(2,1)S(1)}, u32[]{:S(2)}, u32[]{:S(2)}) collective-permute-start(bf16[256,512]{1,0:T(8,128)(2,1)S(1)} %get-tuple-element.50), channel_id=1, source_target_pairs={{0,24},{8,0},{16,8},{24,16},{1,25},{9,1},{17,9},{25,17},{2,26},{10... | collective-permute-start | bytes 786440 | tf_op jit(solution)/shard_map/ppermute | solution.py:348
  661.7 30.5 %collective-permute-start.29 = (bf16[256,512]{1,0:T(8,128)(2,1)S(1)}, bf16[256,512]{1,0:T(8,128)(2,1)S(1)}, u32[]{:S(2)}, u32[]{:S(2)}) collective-permute-start(bf16[256,512]{1,0:T(8,128)(2,1)S(1)} %get-tuple-element.51), channel_id=1, source_target_pairs={{0,16},{8,24},{16,0},{24,8},{1,17},{9,25},{17,1},{25,9},{2,18},{10... | collective-permute-start | bytes 786440 | tf_op jit(solution)/shard_map/ppermute | solution.py:348
  664.6 27.6 %collective-permute-start.30 = (bf16[256,512]{1,0:T(8,128)(2,1)S(1)}, bf16[256,512]{1,0:T(8,128)(2,1)S(1)}, u32[]{:S(2)}, u32[]{:S(2)}) collective-permute-start(bf16[256,512]{1,0:T(8,128)(2,1)S(1)} %get-tuple-element.52), channel_id=1, source_target_pairs={{0,8},{8,16},{16,24},{24,0},{1,9},{9,17},{17,25},{25,1},{2,10},{10... | collective-permute-start | bytes 786440 | tf_op jit(solution)/shard_map/ppermute | solution.py:348
  (61 other events, 872.8 us)
